TPU v7x, 256 devices: a whole 4x4x8 slice. The times are simulated.
256 devices in a mesh: band: 4 (over z_hi), fft: 64 (over y, z_lo, x, core).
Axes of the slice: x: 4, y: 4, z: 8 (z_hi: 4, z_lo: 2; z = z_hi * 2 + z_lo), core: 2. Of those that a mesh axis runs over, the one named last changes fastest.
Arguments:
- psi: float32 [2, 4, 160, 16384], P(None, 'band', None, 'fft'), may hold values from -8 to 8
- potential: float32 [320, 320, 320], P('fft'), may hold values from -5 to 5
- stick_columns: int32 [16384], replicated, may hold values from 0 to 25599, as said below
Outputs:
- hpsi: float32 [2, 4, 160, 16384], P(None, 'band', None, 'fft')
- margin: float32 [2, 4, 4], P(None, None, 'band')
Inputs may be any that keep to these rules, and one draw needn't show every extreme that they name: `stick_columns`: distinct values.
All inputs are finite; a program needn't handle non-finite values.
Results may differ from a plain program's by a relative error of at most 0.000077.
Values sent between devices are 32-bit elements; how exact they have to be, the bound alone decides.
A program may use at most 128 MiB of HBM per device.

v0:
```python
import functools
import math

import jax
import jax.numpy as jnp
import numpy as np
from jax import lax
from jax.experimental import pallas as pl
from jax.experimental.pallas import tpu as pltpu
from jax.sharding import PartitionSpec as P

LANES = 128
ROWS = 16


def dft_tables(grid_size, freq_count):
    points = np.arange(grid_size)[:, None]
    freqs = np.arange(freq_count)[None, :] - freq_count // 2
    angle = (points * freqs % grid_size).astype(np.float64) * (2.0 * math.pi / grid_size)
    return np.cos(angle).astype(np.float32), np.sin(angle).astype(np.float32)


def halves(table):
    high = table.astype(jnp.bfloat16)
    low = (table - high.astype(np.float32)).astype(jnp.bfloat16)
    return high, low


def split(value):
    high = value.astype(jnp.bfloat16)
    low = (value - high.astype(jnp.float32)).astype(jnp.bfloat16)
    return high, low


def dot(left, right):
    return jnp.dot(left, right, preferred_element_type=jnp.float32)


def plane_tables(cosine, sine, chunk):
    grid, freqs = cosine.shape
    wide = -(-grid // LANES) * LANES
    wide_v = -(-freqs // LANES) * LANES
    y_out = np.zeros((freqs, 2 * wide), np.float32)
    y_out[:, :grid] = cosine.T
    y_out[:, wide : wide + grid] = sine.T
    y_back = np.zeros((wide, 2 * wide_v), np.float32)
    y_back[:grid, :freqs] = cosine
    y_back[:grid, wide_v : wide_v + freqs] = sine
    x_out = np.stack([cosine.reshape(grid // chunk, chunk, freqs), sine.reshape(grid // chunk, chunk, freqs)], axis=1)
    x_high, x_low = halves(x_out.reshape(2 * grid, freqs))
    x_out = np.concatenate([x_high, x_low, x_high], axis=1)
    b_high, b_low = halves(np.concatenate([cosine.T, sine.T], axis=0))
    x_back = np.concatenate([b_high, b_low, b_high], axis=1)
    return (*halves(y_out), x_out, x_back, *halves(y_back))


def plane_kernel(
    chunk,
    columns,
    recv,
    potential,
    y_out_high,
    y_out_low,
    x_out,
    x_back,
    y_back_high,
    y_back_low,
    send,
    sticks,
    grid_rows,
    flat,
    planes,
    right_x,
    right_b,
):
    planes_held, grid, _ = potential.shape
    freqs = y_out_high.shape[0]
    wide = y_out_high.shape[1] // 2
    wide_v = y_back_high.shape[1] // 2
    blocks = recv.shape[0]
    values = 2 * planes_held
    total = columns.shape[0]
    unroll = 64

    def clear(i, _):
        grid_rows[pl.ds(i * freqs, freqs), :] = jnp.zeros((freqs, LANES), jnp.float32)
        return 0

    lax.fori_loop(0, freqs, clear, 0)
    right_b[...] = jnp.zeros_like(right_b)

    def to_rows(i, _):
        block = jnp.concatenate([recv[i, k] for k in range(recv.shape[1])], axis=0)
        block = jnp.concatenate([block, jnp.zeros((LANES - block.shape[0], LANES), jnp.float32)], axis=0)
        turned = block.T
        sticks[pl.ds(i * 2 * LANES, LANES), :] = turned
        sticks[pl.ds(i * 2 * LANES + LANES, LANES), :] = pltpu.roll(turned, LANES - values, 1)
        return 0

    lax.fori_loop(0, blocks, to_rows, 0)

    def scatter(i, _):
        base = i * unroll
        rows = [sticks[pl.ds(base + j, 1), :] for j in range(unroll)]
        for j in range(unroll):
            grid_rows[pl.ds(columns[base + j], 1), :] = rows[j]
        return 0

    lax.fori_loop(0, total // unroll, scatter, 0)

    def to_planes(u, _):
        turned = grid_rows[pl.ds(u * freqs, freqs), :].T
        for k in range(flat.shape[0]):
            upper = min(freqs - k * LANES, LANES)
            flat[k, pl.ds(u * ROWS, ROWS), 0:upper] = turned[0:ROWS, k * LANES : k * LANES + upper]
        return 0

    lax.fori_loop(0, freqs, to_planes, 0)

    def plane(z, _):
        real, imag = (
            jnp.concatenate([flat[k, pl.ds(at, freqs, stride=ROWS), :] for k in range(flat.shape[0])], axis=1)[:, :freqs]
            for at in (z, planes_held + z)
        )
        high, low = split(jnp.concatenate([real, imag], axis=0))
        prod = dot(high, y_out_high[...]) + dot(low, y_out_high[...]) + dot(high, y_out_low[...])
        along_re = prod[:freqs, :wide] - prod[freqs:, wide:]
        along_im = prod[:freqs, wide:] + prod[freqs:, :wide]
        high, low = split(jnp.concatenate([along_re, along_im], axis=1))
        right_x[0:freqs, :] = high
        right_x[freqs : 2 * freqs, :] = high
        right_x[2 * freqs : 3 * freqs, :] = low

        def part(i, _):
            prod = dot(x_out[pl.ds(i * 2 * chunk, 2 * chunk), :], right_x[...])
            here = potential[z, pl.ds(i * chunk, chunk), :]
            real = (prod[:chunk, :wide] - prod[chunk:, wide:])[:, :grid] * here
            imag = (prod[:chunk, wide:] + prod[chunk:, :wide])[:, :grid] * here
            for value, at in ((real, 0), (imag, wide)):
                high, low = split(value)
                right_b[pl.ds(i * chunk, chunk), at : at + grid] = high
                right_b[pl.ds(grid + i * chunk, chunk), at : at + grid] = high
                right_b[pl.ds(2 * grid + i * chunk, chunk), at : at + grid] = low
            return 0

        lax.fori_loop(0, grid // chunk, part, 0)
        prod = dot(x_back[...], right_b[...])
        back_re = prod[:freqs, :wide] + prod[freqs:, wide:]
        back_im = prod[:freqs, wide:] - prod[freqs:, :wide]
        high, low = split(jnp.concatenate([back_re, back_im], axis=0))
        prod = dot(high, y_back_high[...]) + dot(low, y_back_high[...]) + dot(high, y_back_low[...])
        done_re = prod[:freqs, :wide_v] + prod[freqs:, wide_v:]
        done_im = prod[freqs:, :wide_v] - prod[:freqs, wide_v:]
        for k in range(planes.shape[0]):
            planes[k, pl.ds(z * freqs, freqs), :] = done_re[:, k * LANES : (k + 1) * LANES]
            planes[k, pl.ds((planes_held + z) * freqs, freqs), :] = done_im[:, k * LANES : (k + 1) * LANES]
        return 0

    lax.fori_loop(0, planes_held, plane, 0)

    def from_planes(u, _):
        for k in range(planes.shape[0]):
            upper = min(freqs - k * LANES, LANES)
            turned = planes[k, pl.ds(u, ROWS, stride=freqs), :].T
            grid_rows[pl.ds(u * freqs + k * LANES, upper), 0:ROWS] = turned[:upper]
        return 0

    lax.fori_loop(0, freqs, from_planes, 0)

    def gather(i, _):
        base = i * unroll
        rows = [grid_rows[pl.ds(columns[base + j], 1), :] for j in range(unroll)]
        for j in range(unroll):
            sticks[pl.ds(base + j, 1), :] = rows[j]
        return 0

    lax.fori_loop(0, total // unroll, gather, 0)

    def from_rows(i, _):
        first = sticks[pl.ds(i * 2 * LANES, LANES), :].T[:values]
        second = sticks[pl.ds(i * 2 * LANES + LANES, LANES), :].T[:values]
        block = jnp.concatenate([first, second], axis=0)
        depth = send.shape[2]
        for k in range(send.shape[1]):
            send[i, k] = block[k * depth : (k + 1) * depth]
        return 0

    lax.fori_loop(0, blocks, from_rows, 0)


def plane_call(recv, potential, columns, cosine, sine):
    planes_held, grid, _ = potential.shape
    freqs = cosine.shape[1]
    chunk = 64
    tables = plane_tables(cosine, sine, chunk)
    wide = tables[0].shape[1] // 2
    wide_v = tables[4].shape[1] // 2
    vmem = pl.BlockSpec(memory_space=pltpu.VMEM)
    return pl.pallas_call(
        functools.partial(plane_kernel, chunk),
        out_shape=jax.ShapeDtypeStruct(recv.shape, jnp.float32),
        in_specs=[pl.BlockSpec(memory_space=pltpu.SMEM)] + [vmem] * 8,
        out_specs=vmem,
        scratch_shapes=[
            pltpu.VMEM((columns.shape[0], LANES), jnp.float32),
            pltpu.VMEM((freqs * freqs, LANES), jnp.float32),
            pltpu.VMEM((wide_v // LANES, freqs * ROWS, LANES), jnp.float32),
            pltpu.VMEM((wide_v // LANES, ROWS * freqs, LANES), jnp.float32),
            pltpu.VMEM((3 * freqs, 2 * wide), jnp.bfloat16),
            pltpu.VMEM((3 * grid, 2 * wide), jnp.bfloat16),
        ],
        compiler_params=pltpu.CompilerParams(vmem_limit_bytes=56 * 1024 * 1024),
        name="planes",
    )(columns, recv, potential, *tables)


def kinetic_factors(columns, freq_count):
    centre = freq_count // 2
    along_u = columns // freq_count - centre
    along_v = columns % freq_count - centre
    along_w = jnp.arange(freq_count, dtype=jnp.int32) - centre
    squared = along_w[:, None] * along_w[:, None] + (along_u * along_u + along_v * along_v)[None, :]
    return 0.5 * squared.astype(jnp.float32) / float(centre * centre)


def margin_of(left, right):
    high = lax.Precision.HIGHEST
    real_part = jnp.einsum("mws,nws->mn", left[0], right[0], precision=high) + jnp.einsum(
        "mws,nws->mn", left[1], right[1], precision=high
    )
    imag_part = jnp.einsum("mws,nws->mn", left[0], right[1], precision=high) - jnp.einsum(
        "mws,nws->mn", left[1], right[0], precision=high
    )
    return jnp.stack([real_part, imag_part])


def on_device(psi, potential, stick_columns):
    freq_count = psi.shape[2]
    per_device = psi.shape[3]
    grid_size = potential.shape[1]
    plane_count = potential.shape[0]
    fft_count = lax.axis_size("fft")
    position = lax.axis_index("fft")
    cosine, sine = dft_tables(grid_size, freq_count)
    table = np.stack([np.stack([cosine, -sine], 1), np.stack([sine, cosine], 1)])
    table = table.reshape(2, fft_count, plane_count, 2 * freq_count).transpose(1, 0, 2, 3)
    table = table.reshape(fft_count * 2 * plane_count, 2 * freq_count)
    my_columns = lax.dynamic_slice_in_dim(stick_columns, position * per_device, per_device)
    sent = jnp.dot(table, psi.reshape(2 * freq_count, per_device), precision=lax.Precision.HIGH)
    halves_of = per_device // LANES
    sent = sent.reshape(fft_count, 2 * plane_count, halves_of, LANES).transpose(0, 2, 1, 3)
    sent = sent.reshape(fft_count, plane_count, 4, LANES)
    moved = lax.all_to_all(sent, "fft", split_axis=0, concat_axis=0, tiled=True)
    picked = plane_call(moved, potential, stick_columns, cosine, sine)
    returned = lax.all_to_all(picked, "fft", split_axis=0, concat_axis=0, tiled=True)
    returned = returned.reshape(fft_count, halves_of, 2 * plane_count, LANES).transpose(0, 2, 1, 3)
    returned = returned.reshape(fft_count * 2 * plane_count, per_device)
    applied = jnp.dot(table.T, returned, precision=lax.Precision.HIGH).reshape(psi.shape)
    kinetic = kinetic_factors(my_columns, freq_count)
    hpsi = kinetic * psi + applied / float(grid_size * grid_size * grid_size)
    partial_sums = margin_of(lax.all_gather(psi, "band", axis=1, tiled=True), hpsi)
    totals = lax.psum(partial_sums, "fft")
    margin = totals / float(freq_count * per_device * fft_count)
    return (hpsi, margin)


def solution(mesh):
    placed = (P(None, "band", None, "fft"), P("fft", None, None), P())
    return jax.shard_map(
        on_device,
        mesh=mesh,
        in_specs=placed,
        out_specs=(P(None, "band", None, "fft"), P(None, None, "band")),
        check_vma=False,
    )
```

profile of v0, /device:TPU:1, one launch (start us, length us, event | category | flops | bytes accessed | tf_op | source)
XLA Modules:
  0.0 312.6 jit_solution(10751707510097786072)
XLA Ops:
  7.2 1.9 convolution_bitcast_fusion
  9.1 0.1 copy.16
  9.2 1.3 copy.17
  10.4 10.3 %all-to-all-start = ((f32[64,5,4,128]{3,2,1,0:T(4,128)}), f32[64,5,4,128]{3,2,1,0:T(4,128)S(1)}, u32[]{:S(2)}, u32[]{:S(2)}) async-start(f32[64,5,4,128]{3,2,1,0:T(4,128)} %copy.17), calls=%async_computation | async-start | bytes 1310720 | tf_op jit(solution)/shard_map/all_to_all | solution.py:253
  20.8 0.0 all-gather.2.cloned.1.call-start
  20.8 0.7 all-gather.2.cloned.1.call-update
  21.5 13.1 %all-to-all-done.recv = f32[64,5,4,128]{3,2,1,0:T(4,128)S(1)} async-done(((f32[64,5,4,128]{3,2,1,0:T(4,128)}), f32[64,5,4,128]{3,2,1,0:T(4,128)S(1)}, u32[]{:S(2)}, u32[]{:S(2)}) %all-to-all-start) | async-done | bytes 655392 | tf_op jit(solution)/shard_map/all_to_all | solution.py:253
  34.6 0.8 copy-done.1
  35.5 99.3 %planes.1 = f32[64,5,4,128]{3,2,1,0:T(4,128)} custom-call(s32[16384]{0:T(1024)} %columns.1, f32[64,5,4,128]{3,2,1,0:T(4,128)} %copy-done.1, f32[5,320,320]{2,1,0:T(8,128)} %potential.1, bf16[160,768]{1,0:T(8,128)(2,1)} %constant.63.clone.y_out_high, bf16[160,768]{1,0:T(8,128)(2,1)} %constant.64.clone.y_out_low, bf16[640,480]{1,0:T(8,128)(2,1)} %constant.65.clone.x_out, ...), custom_call_target="tpu_custom_call" | custom-call | tf_op jit(solution)/shard_map/planes/pallas_call | solution.py:199
  134.8 4.4 %all-to-all-start.1 = ((f32[64,5,4,128]{3,2,1,0:T(4,128)}), f32[64,5,4,128]{3,2,1,0:T(4,128)S(1)}, u32[]{:S(2)}, u32[]{:S(2)}) async-start(f32[64,5,4,128]{3,2,1,0:T(4,128)} %planes.1), calls=%async_computation.1 | async-start | bytes 1310720 | tf_op jit(solution)/shard_map/all_to_all | solution.py:255
  139.2 0.8 fusion.17
  140.0 0.1 convert_multiply_fusion
  140.1 1.4 slice_bitcast_fusion.1
  141.6 11.6 %all-to-all-done.1 = f32[64,5,4,128]{3,2,1,0:T(4,128)S(1)} async-done(((f32[64,5,4,128]{3,2,1,0:T(4,128)}), f32[64,5,4,128]{3,2,1,0:T(4,128)S(1)}, u32[]{:S(2)}, u32[]{:S(2)}) %all-to-all-start.1) | async-done | bytes 655392 | tf_op jit(solution)/shard_map/all_to_all | solution.py:255
  153.2 0.1 copy.18
  153.2 0.5 copy.19
  153.8 0.6 convolution_multiply_fusion
  154.4 0.1 multiply_add_fusion
  154.5 3.1 %convolution_bitcast_fusion.3 = f32[4]{0:T(128)S(1)} fusion(f32[4,160,256]{2,1,0:T(8,128)S(1)} %get-tuple-element.3, f32[160,256,1]{1,0,2:T(8,128)S(1)} %get-tuple-element.4), kind=kOutput, calls=%fused_computation.4 | convolution fusion | flops 1966080 | bytes 819216 | tf_op jit(solution)/shard_map/mws,nws->mn/dot_general | solution.py:228
  157.6 3.2 %convolution_bitcast_fusion.1 = f32[4]{0:T(128)S(1)} fusion(f32[4,160,256]{2,1,0:T(8,128)S(1)} %get-tuple-element.3, f32[160,256,1]{1,0,2:T(8,128)S(1)} %get-tuple-element.5), kind=kOutput, calls=%fused_computation.2 | convolution fusion | flops 1966080 | bytes 819216 | tf_op jit(solution)/shard_map/mws,nws->mn/dot_general | solution.py:231
  160.8 3.0 fusion.1
  163.8 3.2 %fusion.3 = f32[1,4,1]{1,2,0:T(1,128)S(1)} fusion(f32[4]{0:T(128)S(1)} %convolution_bitcast_fusion.1, f32[4,160,256]{2,1,0:T(8,128)S(1)} %get-tuple-element.2, f32[160,256,1]{1,0,2:T(8,128)S(1)} %get-tuple-element.4), kind=kOutput, calls=%fused_computation.9 | convolution fusion | flops 1966084 | bytes 819232 | tf_op jit(solution)/shard_map/mws,nws->mn/dot_general | solution.py:231
  167.0 138.2 %psum.7 = f32[2,4,1]{1,2,0:T(1,128)S(1)} all-reduce(f32[2,4,1]{1,2,0:T(1,128)S(1)} %pad_maximum_fusion), channel_id=1, replica_groups=mesh['band'=4,'fft'=64] {'fft'}, use_global_device_ids=true, to_apply=%region_0.1 | all-reduce | flops 8 | bytes 64 | tf_op jit(solution)/shard_map/psum | solution.py:262
  305.2 0.6 broadcast_multiply_fusion
  (11 shorter events, 0.1 us)
Async XLA Ops:
  10.4 24.2 %all-to-all-start = ((f32[64,5,4,128]{3,2,1,0:T(4,128)}), f32[64,5,4,128]{3,2,1,0:T(4,128)S(1)}, u32[]{:S(2)}, u32[]{:S(2)}) async-start(f32[64,5,4,128]{3,2,1,0:T(4,128)} %copy.17), calls=%async_computation | async-start | bytes 1310720 | tf_op jit(solution)/shard_map/all_to_all | solution.py:253
  20.8 119.3 %all-gather.2.cloned.1.call-start = ((), (), s32[]{:S(2)}) async-start(), calls=%async_computation.2 | async-start | bytes 1638400 | tf_op jit(solution)/shard_map/all_gather | solution.py:261
  34.6 0.8 copy-start.1
  134.8 18.4 %all-to-all-start.1 = ((f32[64,5,4,128]{3,2,1,0:T(4,128)}), f32[64,5,4,128]{3,2,1,0:T(4,128)S(1)}, u32[]{:S(2)}, u32[]{:S(2)}) async-start(f32[64,5,4,128]{3,2,1,0:T(4,128)} %planes.1), calls=%async_computation.1 | async-start | bytes 1310720 | tf_op jit(solution)/shard_map/all_to_all | solution.py:255
  141.6 12.2 %copy-start.3 = (f32[320,640]{1,0:T(8,128)S(1)}, f32[320,640]{1,0:T(8,128)}, u32[]{:S(2)}) copy-start(f32[320,640]{1,0:T(8,128)} %constant.69.clone) | copy-start | bytes 2457604
  153.2 1.1 copy-start
  154.4 6.4 %copy-start.2 = (f32[2,1,160,256]{3,2,1,0:T(8,128)}, f32[2,1,160,256]{3,2,1,0:T(8,128)S(1)}, u32[]{:S(2)}) copy-start(f32[2,1,160,256]{3,2,1,0:T(8,128)S(1)} %multiply_add_fusion) | copy-start | bytes 983044
Sparse Core Ops, SparseCore 0:
  23.4 40.4 all-gather.1
where the time goes:
time: 313 us
  blocking collectives  138 us (44%)
  Pallas kernels  99.3 us (32%)
  waiting for transfers between devices  25.4 us (8%)
  matrix products  15 us (5%)
  starting transfers between devices  14.8 us (5%)
  between operations  14.2 us (5%)
  local copies, waits for them, and re-layouts  4.21 us (1%)
    psum x1, blocking collectives, on_device(): totals = lax.psum(partial_sums, 'fft')  138 us
    pallas_call x1, Pallas kernels, plane_call(): pl.pallas_call(functools.partial(plane_kernel, chunk), out_shape=jax.Shap...  99.3 us
    all_to_all x1, waiting for transfers between devices, on_device(): moved = lax.all_to_all(sent, 'fft', split_axis=0, concat_axis=0, tiled=True)  13.1 us
    all_to_all x1, waiting for transfers between devices, on_device(): lax.all_to_all(picked, 'fft', split_axis=0, concat_axis=0, tiled=True)  11.6 us
    all_to_all x1, starting transfers between devices, on_device(): moved = lax.all_to_all(sent, 'fft', split_axis=0, concat_axis=0, tiled=True)  10.3 us
  transfers between devices with their start and end apart: 3, of which 2 were waited for; matrix products, arithmetic and copies ran while one was open for 1% of the time, Pallas kernels for 32%

commit v1 on v0

--- a/solution.py
+++ b/solution.py
@@ -11,6 +11,7 @@
 
 LANES = 128
 ROWS = 16
+MESH = pl.DeviceIdType.MESH
 
 
 def dft_tables(grid_size, freq_count):
@@ -97,7 +98,7 @@
         sticks[pl.ds(i * 2 * LANES + LANES, LANES), :] = pltpu.roll(turned, LANES - values, 1)
         return 0
 
-    lax.fori_loop(0, blocks, to_rows, 0)
+    lax.fori_loop(0, blocks, to_rows, 0, unroll=4)
 
     def scatter(i, _):
         base = i * unroll
@@ -115,7 +116,7 @@
             flat[k, pl.ds(u * ROWS, ROWS), 0:upper] = turned[0:ROWS, k * LANES : k * LANES + upper]
         return 0
 
-    lax.fori_loop(0, freqs, to_planes, 0)
+    lax.fori_loop(0, freqs, to_planes, 0, unroll=8)
 
     def plane(z, _):
         real, imag = (
@@ -165,7 +166,7 @@
             grid_rows[pl.ds(u * freqs + k * LANES, upper), 0:ROWS] = turned[:upper]
         return 0
 
-    lax.fori_loop(0, freqs, from_planes, 0)
+    lax.fori_loop(0, freqs, from_planes, 0, unroll=8)
 
     def gather(i, _):
         base = i * unroll
@@ -185,7 +186,7 @@
             send[i, k] = block[k * depth : (k + 1) * depth]
         return 0
 
-    lax.fori_loop(0, blocks, from_rows, 0)
+    lax.fori_loop(0, blocks, from_rows, 0, unroll=4)
 
 
 def plane_call(recv, potential, columns, cosine, sine):
@@ -223,15 +224,188 @@
     return 0.5 * squared.astype(jnp.float32) / float(centre * centre)
 
 
-def margin_of(left, right):
-    high = lax.Precision.HIGHEST
-    real_part = jnp.einsum("mws,nws->mn", left[0], right[0], precision=high) + jnp.einsum(
-        "mws,nws->mn", left[1], right[1], precision=high
-    )
-    imag_part = jnp.einsum("mws,nws->mn", left[0], right[1], precision=high) - jnp.einsum(
-        "mws,nws->mn", left[1], right[0], precision=high
-    )
-    return jnp.stack([real_part, imag_part])
+def greet(position, count):
+    barrier = pltpu.get_barrier_semaphore()
+
+    def signal(k, _):
+        pl.semaphore_signal(barrier, inc=1, device_id={"fft": lax.rem(position + k, count)}, device_id_type=MESH)
+        return 0
+
+    lax.fori_loop(1, count, signal, 0)
+    return barrier
+
+
+def await_others(buffer, semaphore):
+    others = buffer.at[pl.ds(0, buffer.shape[0] - 1)]
+    pltpu.make_async_copy(others, others, semaphore).wait()
+
+
+def spread_kernel(psi, table_high, table_low, recv, staged, send, send_sem, recv_sem):
+    count, pieces, depth, _ = recv.shape
+    values = pieces * depth // 2
+    position = lax.axis_index("fft")
+    barrier = greet(position, count)
+    high, low = split(psi[...])
+    staged[...] = dot(table_high[...], high) + dot(table_low[...], high) + dot(table_high[...], low)
+    pl.semaphore_wait(barrier, count - 1)
+
+    def stage(peer):
+        rows = staged[pl.ds(peer * ROWS, ROWS), :]
+        block = jnp.concatenate([rows[:values, :LANES], rows[:values, LANES:]], axis=0)
+        return [block[k * depth : (k + 1) * depth] for k in range(pieces)]
+
+    def post(k, _):
+        peer = lax.rem(position + k, count)
+        for at, piece in enumerate(stage(peer)):
+            send[peer, at] = piece
+        pltpu.make_async_remote_copy(
+            src_ref=send.at[peer],
+            dst_ref=recv.at[position],
+            send_sem=send_sem,
+            recv_sem=recv_sem,
+            device_id={"fft": peer},
+            device_id_type=MESH,
+        ).start()
+        return 0
+
+    lax.fori_loop(1, count, post, 0)
+    for at, piece in enumerate(stage(position)):
+        recv[position, at] = piece
+    await_others(recv, recv_sem)
+    await_others(recv, send_sem)
+
+
+def spread_call(psi, table, count, planes_held):
+    rows = table.shape[0]
+    vmem = pl.BlockSpec(memory_space=pltpu.VMEM)
+    shape = (count, planes_held, 2 * psi.shape[1] // LANES, LANES)
+    return pl.pallas_call(
+        spread_kernel,
+        out_shape=jax.ShapeDtypeStruct(shape, jnp.float32),
+        in_specs=[vmem] * 3,
+        out_specs=vmem,
+        scratch_shapes=[
+            pltpu.VMEM((rows, psi.shape[1]), jnp.float32),
+            pltpu.VMEM(shape, jnp.float32),
+            pltpu.SemaphoreType.DMA,
+            pltpu.SemaphoreType.DMA,
+        ],
+        compiler_params=pltpu.CompilerParams(
+            collective_id=0, has_side_effects=True, vmem_limit_bytes=32 * 1024 * 1024
+        ),
+        name="spread",
+    )(psi, *halves(table))
+
+
+def collect_kernel(
+    scale,
+    weight,
+    picked,
+    psi,
+    bands,
+    kinetic,
+    table_high,
+    table_low,
+    hpsi,
+    margin,
+    got,
+    right,
+    sums,
+    send_sem,
+    recv_sem,
+    sum_send_sem,
+    sum_recv_sem,
+):
+    count, pieces, depth, _ = picked.shape
+    values = pieces * depth // 2
+    freqs = kinetic.shape[0]
+    position = lax.axis_index("fft")
+    barrier = greet(position, count)
+    pl.semaphore_wait(barrier, count - 1)
+
+    def post(k, _):
+        peer = lax.rem(position + k, count)
+        pltpu.make_async_remote_copy(
+            src_ref=picked.at[peer],
+            dst_ref=got.at[position],
+            send_sem=send_sem,
+            recv_sem=recv_sem,
+            device_id={"fft": peer},
+            device_id_type=MESH,
+        ).start()
+        return 0
+
+    lax.fori_loop(1, count, post, 0)
+    got[position] = picked[position]
+    await_others(got, recv_sem)
+
+    def to_right(i, _):
+        block = jnp.concatenate([got[i, k] for k in range(pieces)], axis=0)
+        blank = jnp.zeros((ROWS - values, LANES), jnp.float32)
+        at = pl.multiple_of(i * ROWS, ROWS)
+        right[pl.ds(at, ROWS), 0:LANES] = jnp.concatenate([block[:values], blank], axis=0)
+        right[pl.ds(at, ROWS), LANES : 2 * LANES] = jnp.concatenate([block[values:], blank], axis=0)
+        return 0
+
+    lax.fori_loop(0, count, to_right, 0, unroll=4)
+    high, low = split(right[...])
+    applied = dot(table_high[...], high) + dot(table_low[...], high) + dot(table_high[...], low)
+    hpsi[0:freqs, :] = kinetic[...] * psi[0:freqs, :] + applied[:freqs] * scale
+    hpsi[freqs : 2 * freqs, :] = kinetic[...] * psi[freqs : 2 * freqs, :] + applied[freqs:] * scale
+
+    def folded(product):
+        narrow = product[:, :LANES] + product[:, LANES:]
+        return jnp.sum(narrow, axis=0, keepdims=True)
+
+    real_rows, imag_rows = [], []
+    for m in range(bands.shape[0]):
+        left_re, left_im = bands[m, 0:freqs, :], bands[m, freqs : 2 * freqs, :]
+        right_re, right_im = hpsi[0:freqs, :], hpsi[freqs : 2 * freqs, :]
+        real_rows.append(folded(left_re * right_re + left_im * right_im))
+        imag_rows.append(folded(left_re * right_im - left_im * right_re))
+    sums[position] = jnp.concatenate(real_rows + imag_rows, axis=0) * weight
+
+    def post_sums(k, _):
+        pltpu.make_async_remote_copy(
+            src_ref=sums.at[position],
+            dst_ref=sums.at[position],
+            send_sem=sum_send_sem,
+            recv_sem=sum_recv_sem,
+            device_id={"fft": lax.rem(position + k, count)},
+            device_id_type=MESH,
+        ).start()
+        return 0
+
+    lax.fori_loop(1, count, post_sums, 0)
+    await_others(sums, sum_recv_sem)
+    margin[...] = jnp.sum(jnp.sum(sums[...], axis=0), axis=1, keepdims=True)
+    await_others(got, send_sem)
+    await_others(sums, sum_send_sem)
+
+
+def collect_call(picked, psi, bands, kinetic, table, scale, weight):
+    count = picked.shape[0]
+    vmem = pl.BlockSpec(memory_space=pltpu.VMEM)
+    height = 2 * bands.shape[0]
+    return pl.pallas_call(
+        functools.partial(collect_kernel, scale, weight),
+        out_shape=(jax.ShapeDtypeStruct(psi.shape, jnp.float32), jax.ShapeDtypeStruct((height, 1), jnp.float32)),
+        in_specs=[vmem] * 6,
+        out_specs=(vmem, vmem),
+        scratch_shapes=[
+            pltpu.VMEM(picked.shape, jnp.float32),
+            pltpu.VMEM((count * ROWS, psi.shape[1]), jnp.float32),
+            pltpu.VMEM((count, height, LANES), jnp.float32),
+            pltpu.SemaphoreType.DMA,
+            pltpu.SemaphoreType.DMA,
+            pltpu.SemaphoreType.DMA,
+            pltpu.SemaphoreType.DMA,
+        ],
+        compiler_params=pltpu.CompilerParams(
+            collective_id=1, has_side_effects=True, vmem_limit_bytes=32 * 1024 * 1024
+        ),
+        name="collect",
+    )(picked, psi, bands, kinetic, *halves(table.T))
 
 
 def on_device(psi, potential, stick_columns):
@@ -242,26 +416,20 @@
     fft_count = lax.axis_size("fft")
     position = lax.axis_index("fft")
     cosine, sine = dft_tables(grid_size, freq_count)
-    table = np.stack([np.stack([cosine, -sine], 1), np.stack([sine, cosine], 1)])
+    table = np.stack([np.concatenate([cosine, -sine], 1), np.concatenate([sine, cosine], 1)])
     table = table.reshape(2, fft_count, plane_count, 2 * freq_count).transpose(1, 0, 2, 3)
-    table = table.reshape(fft_count * 2 * plane_count, 2 * freq_count)
+    table = table.reshape(fft_count, 2 * plane_count, 2 * freq_count)
+    table = np.pad(table, ((0, 0), (0, ROWS - 2 * plane_count), (0, 0))).reshape(fft_count * ROWS, 2 * freq_count)
+    flat_psi = psi.reshape(2 * freq_count, per_device)
+    moved = spread_call(flat_psi, table, fft_count, plane_count)
+    picked = plane_call(moved, potential, stick_columns, cosine, sine)
+    bands = lax.all_gather(flat_psi, "band", axis=0)
     my_columns = lax.dynamic_slice_in_dim(stick_columns, position * per_device, per_device)
-    sent = jnp.dot(table, psi.reshape(2 * freq_count, per_device), precision=lax.Precision.HIGH)
-    halves_of = per_device // LANES
-    sent = sent.reshape(fft_count, 2 * plane_count, halves_of, LANES).transpose(0, 2, 1, 3)
-    sent = sent.reshape(fft_count, plane_count, 4, LANES)
-    moved = lax.all_to_all(sent, "fft", split_axis=0, concat_axis=0, tiled=True)
-    picked = plane_call(moved, potential, stick_columns, cosine, sine)
-    returned = lax.all_to_all(picked, "fft", split_axis=0, concat_axis=0, tiled=True)
-    returned = returned.reshape(fft_count, halves_of, 2 * plane_count, LANES).transpose(0, 2, 1, 3)
-    returned = returned.reshape(fft_count * 2 * plane_count, per_device)
-    applied = jnp.dot(table.T, returned, precision=lax.Precision.HIGH).reshape(psi.shape)
     kinetic = kinetic_factors(my_columns, freq_count)
-    hpsi = kinetic * psi + applied / float(grid_size * grid_size * grid_size)
-    partial_sums = margin_of(lax.all_gather(psi, "band", axis=1, tiled=True), hpsi)
-    totals = lax.psum(partial_sums, "fft")
-    margin = totals / float(freq_count * per_device * fft_count)
-    return (hpsi, margin)
+    scale = 1.0 / float(grid_size * grid_size * grid_size)
+    weight = 1.0 / float(freq_count * per_device * fft_count)
+    hpsi, margin = collect_call(picked, flat_psi, bands, kinetic, table, scale, weight)
+    return (hpsi.reshape(psi.shape), margin.reshape(2, bands.shape[0], 1))
 
 
 def solution(mesh):

time: 313 us -> 141 us (0.45)
  the two profiles are of different devices: /device:TPU:1 before, /device:TPU:225 now
where the time goes in v1:
time: 141 us; the launch traced here: 140 us
  Pallas kernels  117 us (83%)
  between operations  14.1 us (10%)
  local copies, waits for them, and re-layouts  7.86 us (6%)
    pallas_call x1, Pallas kernels, plane_call(): pl.pallas_call(functools.partial(plane_kernel, chunk), out_shape=jax.Shap...  70.9 us
    pallas_call x1, Pallas kernels, collect_call(): pl.pallas_call(functools.partial(collect_kernel, scale, weight), out_shap...  26.1 us
    pallas_call x1, Pallas kernels, spread_call(): pl.pallas_call(spread_kernel, out_shape=jax.ShapeDtypeStruct(shape, jnp.f...  19.6 us
    unnamed x19, local copies, waits for them, and re-layouts  7.21 us
  transfers between devices with their start and end apart: 1, of which 0 were waited for; matrix products, arithmetic and copies ran while one was open for 1% of the time, Pallas kernels for 64%

profile of v1, /device:TPU:225, one launch (start us, length us, event | category | flops | bytes accessed | tf_op | source)
XLA Modules:
  0.0 140.3 jit_solution(12389237694102037718)
XLA Ops:
  7.2 0.0 all-gather.2.cloned.1.call-start
  7.2 0.7 all-gather.2.cloned.1.call-update
  7.9 0.0 copy-start
  7.9 1.0 copy-done
  8.9 0.0 copy-start.5
  8.9 1.1 copy-done.5
  10.0 1.1 copy-done.6
  11.1 19.6 %spread.1.recv = f32[64,5,4,128]{3,2,1,0:T(4,128)S(1)} custom-call(f32[320,256]{1,0:T(8,128)S(1)} %bitcast.7, bf16[1024,320]{1,0:T(8,128)(2,1)S(1)} %copy-done.5, bf16[1024,320]{1,0:T(8,128)(2,1)S(1)} %copy-done.6), custom_call_target="tpu_custom_call" | custom-call | tf_op jit(solution)/shard_map/spread/pallas_call | solution.py:282
  30.7 0.0 copy-start.3
  30.7 0.8 copy-done.3
  31.6 70.9 %planes.1.picked = f32[64,5,4,128]{3,2,1,0:T(4,128)} custom-call(s32[16384]{0:T(1024)} %columns.1, f32[64,5,4,128]{3,2,1,0:T(4,128)} %copy-done.3, f32[5,320,320]{2,1,0:T(8,128)} %potential.1, bf16[160,768]{1,0:T(8,128)(2,1)} %constant.62.clone.y_out_high, bf16[160,768]{1,0:T(8,128)(2,1)} %constant.63.clone.y_out_low, ...), custom_call_target="tpu_custom_call" | custom-call | tf_op jit(solution)/shard_map/planes/pallas_call | solution.py:200
  102.5 0.8 fusion.2
  103.3 0.1 convert_multiply_fusion.kinetic
  103.4 0.0 all-gather.2.cloned.1.call-done.bands
  103.4 0.0 copy-done.1
  103.4 0.0 copy-done.7
  103.4 0.0 copy-done.8
  103.4 0.0 copy-start.2
  103.4 1.1 copy-done.2
  104.5 1.3 copy-done.4
  105.8 26.1 %collect.1 = (f32[320,256]{1,0:T(8,128)S(1)}, f32[8,1]{1,0:T(8,128)S(1)}) custom-call(f32[64,5,4,128]{3,2,1,0:T(4,128)S(1)} %copy-done.2, f32[320,256]{1,0:T(8,128)S(1)} %bitcast.8, f32[4,320,256]{2,1,0:T(8,128)S(1)} %copy-done.4, f32[160,256]{1,0:T(8,128)S(1)} %convert_multiply_fusion.kinetic, bf16[320,1024]{1,0:T(8,128)(2,1)S(1)} %copy-done.7, ...), custom_call_target="tpu_custom_call" | custom-call | tf_op jit(solution)/shard_map/collect/pallas_call | solution.py:390
  131.9 0.1 reduce
  132.1 0.6 reshape.22
  132.7 0.7 copy.22
  (6 shorter events, 0.0 us)
Async XLA Ops:
  7.2 96.2 %all-gather.2.cloned.1.call-start = ((), (), s32[]{:S(2)}) async-start(), calls=%async_computation | async-start | bytes 1638400 | tf_op jit(solution)/shard_map/all_gather | solution.py:426
  7.9 1.0 copy-start
  8.9 1.1 copy-start.5
  10.0 1.1 copy-start.6
  30.7 0.9 copy-start.3
  31.6 71.8 %copy-start.1 = (f32[2,1,160,256]{3,2,1,0:T(8,128)S(1)}, f32[2,1,160,256]{3,2,1,0:T(8,128)}, u32[]{:S(2)}) copy-start(f32[2,1,160,256]{3,2,1,0:T(8,128)} %param.13) | copy-start | bytes 983044
  31.6 71.8 %copy-start.7 = (bf16[320,1024]{1,0:T(8,128)(2,1)S(1)}, bf16[320,1024]{1,0:T(8,128)(2,1)}, u32[]{:S(2)}) copy-start(bf16[320,1024]{1,0:T(8,128)(2,1)} %constant.68.clone.table_high) | copy-start | bytes 1966084
  31.6 71.8 %copy-start.8 = (bf16[320,1024]{1,0:T(8,128)(2,1)S(1)}, bf16[320,1024]{1,0:T(8,128)(2,1)}, u32[]{:S(2)}) copy-start(bf16[320,1024]{1,0:T(8,128)(2,1)} %constant.69.clone.table_low) | copy-start | bytes 1966084
  103.4 1.1 copy-start.2
  104.5 1.3 copy-start.4
Sparse Core Ops, SparseCore 0:
  9.8 37.7 all-gather.1

commit v2 on v1

v2 whole, which is shorter than its diff:
```python
import functools
import math

import jax
import jax.numpy as jnp
import numpy as np
from jax import lax
from jax.experimental import pallas as pl
from jax.experimental.pallas import tpu as pltpu
from jax.sharding import PartitionSpec as P

LANES = 128
ROWS = 16
MESH = pl.DeviceIdType.MESH


def dft_tables(grid_size, freq_count):
    points = np.arange(grid_size)[:, None]
    freqs = np.arange(freq_count)[None, :] - freq_count // 2
    angle = (points * freqs % grid_size).astype(np.float64) * (2.0 * math.pi / grid_size)
    return np.cos(angle).astype(np.float32), np.sin(angle).astype(np.float32)


def halves(table):
    high = table.astype(jnp.bfloat16)
    low = (table - high.astype(np.float32)).astype(jnp.bfloat16)
    return high, low


def split(value):
    high = value.astype(jnp.bfloat16)
    low = (value - high.astype(jnp.float32)).astype(jnp.bfloat16)
    return high, low


def dot(left, right):
    return jnp.dot(left, right, preferred_element_type=jnp.float32)


def packed_rows(table, whole):
    high, low = halves(table)
    tail = table.shape[0] - whole
    spare = np.zeros((-3 * tail % LANES, table.shape[1]), high.dtype)
    if whole % (2 * LANES) == 0:
        spare = np.zeros((-3 * tail % (2 * LANES), table.shape[1]), high.dtype)
    return np.concatenate([high[:whole], high[:whole], low[:whole], high[whole:], high[whole:], low[whole:], spare], axis=0)


def packed_columns(value, whole, tail):
    high, low = split(value)
    rest_high = high[:, whole : whole + LANES].astype(jnp.float32)
    rest_low = low[:, whole : whole + LANES].astype(jnp.float32)
    parts = [high[:, :whole], low[:, :whole], high[:, :whole]]
    if 3 * tail <= LANES:
        rest = rest_high + pltpu.roll(rest_low, tail, 1) + pltpu.roll(rest_high, 2 * tail, 1)
        parts.append(rest.astype(jnp.bfloat16))
    else:
        parts.append((rest_high + pltpu.roll(rest_low, tail, 1)).astype(jnp.bfloat16))
        parts.append(rest_high.astype(jnp.bfloat16))
    return jnp.concatenate(parts, axis=1)


def three(table):
    high, low = halves(table)
    return np.concatenate([high, low, high], axis=1)


def whole_lanes(count):
    return count // LANES * LANES


def plane_tables(cosine, sine):
    grid, freqs = cosine.shape
    half = grid // 2
    wide = -(-grid // LANES) * LANES
    wide_v = -(-freqs // LANES) * LANES
    y_out = np.zeros((freqs, 2 * wide), np.float32)
    y_out[:, :grid] = cosine.T
    y_out[:, wide : wide + grid] = sine.T
    y_back = np.zeros((grid, 2 * wide_v), np.float32)
    y_back[:, :freqs] = cosine
    y_back[:, wide_v : wide_v + freqs] = sine
    x_out = [three(np.concatenate([cosine[:half, k::2], sine[:half, k::2]], axis=0)) for k in (0, 1)]
    x_back = [three(np.concatenate([cosine[:half, k::2].T, sine[:half, k::2].T], axis=0)) for k in (0, 1)]
    return (
        packed_rows(y_out, whole_lanes(freqs)),
        np.stack(x_out),
        np.stack(x_back),
        packed_rows(y_back, whole_lanes(grid)),
    )


def stacked(value):
    high, low = split(value)
    return jnp.concatenate([high, high, low], axis=0)


def complex_parts(prod, rows, wide, sign):
    real = prod[:rows, :wide] - sign * prod[rows:, wide:]
    imag = prod[:rows, wide:] + sign * prod[rows:, :wide]
    return real, imag


def walk(columns, index, index_sem, visit):
    chunk = index.shape[0] // 2
    pairs = columns.shape[0] // (2 * chunk)

    def fetch(number, slot):
        source = columns.at[pl.ds(pl.multiple_of(number * chunk, chunk), chunk)]
        return pltpu.make_async_copy(source, index.at[pl.ds(slot * chunk, chunk)], index_sem.at[slot])

    fetch(0, 0).start()

    def pair(i, _):
        fetch(2 * i + 1, 1).start()
        fetch(2 * i, 0).wait()
        visit(2 * i * chunk, 0, chunk)

        @pl.when(i < pairs - 1)
        def _():
            fetch(2 * i + 2, 0).start()

        fetch(2 * i + 1, 1).wait()
        visit(2 * i * chunk + chunk, chunk, chunk)
        return 0

    lax.fori_loop(0, pairs, pair, 0)


def plane_kernel(
    columns,
    recv,
    potential_hbm,
    y_out_hbm,
    x_out_hbm,
    x_back_hbm,
    y_back_hbm,
    send,
    sticks,
    grid_rows,
    flat,
    planes,
    potential,
    y_out,
    x_out,
    x_back,
    y_back,
    index,
    load_sem,
    index_sem,
):
    planes_held, grid, _ = potential.shape
    half = grid // 2
    freqs = x_back.shape[1]
    even = freqs // 2
    wide = y_out.shape[1] // 2
    wide_v = y_back.shape[1] // 2
    blocks = recv.shape[0]
    values = 2 * planes_held
    batch = 64

    loads = start_loads(
        (
            (potential_hbm, potential),
            (y_out_hbm, y_out),
            (x_out_hbm, x_out),
            (x_back_hbm, x_back),
            (y_back_hbm, y_back),
        ),
        load_sem,
    )

    def clear(i, _):
        grid_rows[pl.ds(i * freqs, freqs), :] = jnp.zeros((freqs, LANES), jnp.float32)
        return 0

    lax.fori_loop(0, freqs, clear, 0)

    def to_rows(i, _):
        block = jnp.concatenate([recv[i, k] for k in range(recv.shape[1])], axis=0)
        block = jnp.concatenate([block, jnp.zeros((LANES - block.shape[0], LANES), jnp.float32)], axis=0)
        turned = block.T
        sticks[pl.ds(i * 2 * LANES, LANES), :] = turned
        sticks[pl.ds(i * 2 * LANES + LANES, LANES), :] = pltpu.roll(turned, LANES - values, 1)
        return 0

    lax.fori_loop(0, blocks, to_rows, 0, unroll=4)

    def scatter(base, offset, count):
        base = pl.multiple_of(base, count)
        for k in range(0, count, batch):
            rows = [sticks[pl.ds(base + k + j, 1), :] for j in range(batch)]
            for j in range(batch):
                grid_rows[pl.ds(index[offset + k + j], 1), :] = rows[j]

    walk(columns, index, index_sem, scatter)

    def to_planes(u, _):
        turned = grid_rows[pl.ds(u * freqs, freqs), :].T
        for k in range(flat.shape[0]):
            upper = min(freqs - k * LANES, LANES)
            flat[k, pl.ds(u * ROWS, ROWS), 0:upper] = turned[0:ROWS, k * LANES : k * LANES + upper]
        return 0

    lax.fori_loop(0, freqs, to_planes, 0, unroll=8)
    for load in loads:
        load.wait()

    def plane(z, _):
        lane = lax.broadcasted_iota(jnp.int32, (2 * freqs, LANES), 1)
        tiles = []
        for k in range(flat.shape[0]):
            pair = [flat[k, pl.ds(at, freqs, stride=ROWS), :] for at in (z, planes_held + z)]
            pair = jnp.concatenate(pair, axis=0)
            tiles.append(pair if freqs - k * LANES >= LANES else jnp.where(lane < freqs - k * LANES, pair, 0.0))
        left = packed_columns(jnp.concatenate(tiles, axis=1), whole_lanes(freqs), freqs % LANES)
        along = jnp.concatenate(complex_parts(dot(left, y_out[...]), freqs, wide, 1.0), axis=1)
        first_re, first_im = complex_parts(dot(x_out[0], stacked(along[:even])), half, wide, 1.0)
        second_re, second_im = complex_parts(dot(x_out[1], stacked(along[even:])), half, wide, 1.0)
        lower = potential[z, 0:half, :]
        upper = potential[z, half:grid, :]
        blank = jnp.zeros((half, wide - grid), jnp.float32)
        lower = jnp.concatenate([lower, blank], axis=1)
        upper = jnp.concatenate([upper, blank], axis=1)
        low_re, low_im = (first_re + second_re) * lower, (first_im + second_im) * lower
        up_re, up_im = (first_re - second_re) * upper, (first_im - second_im) * upper
        added = jnp.concatenate([low_re + up_re, low_im + up_im], axis=1)
        taken = jnp.concatenate([low_re - up_re, low_im - up_im], axis=1)
        even_re, even_im = complex_parts(dot(x_back[0], stacked(added)), even, wide, -1.0)
        odd_re, odd_im = complex_parts(dot(x_back[1], stacked(taken)), even, wide, -1.0)
        left = packed_columns(
            jnp.concatenate([even_re, odd_re, even_im, odd_im], axis=0), whole_lanes(grid), grid % LANES
        )
        prod = dot(left, y_back[...])
        done_re = prod[:freqs, :wide_v] + prod[freqs:, wide_v:]
        done_im = prod[freqs:, :wide_v] - prod[:freqs, wide_v:]
        for k in range(planes.shape[0]):
            planes[k, pl.ds(z * freqs, freqs), :] = done_re[:, k * LANES : (k + 1) * LANES]
            planes[k, pl.ds((planes_held + z) * freqs, freqs), :] = done_im[:, k * LANES : (k + 1) * LANES]
        return 0

    lax.fori_loop(0, planes_held, plane, 0)

    def from_planes(u, _):
        for k in range(planes.shape[0]):
            upper = min(freqs - k * LANES, LANES)
            turned = planes[k, pl.ds(u, ROWS, stride=freqs), :].T
            grid_rows[pl.ds(u * freqs + k * LANES, upper), 0:ROWS] = turned[:upper]
        return 0

    lax.fori_loop(0, freqs, from_planes, 0, unroll=8)

    def gather(base, offset, count):
        base = pl.multiple_of(base, count)
        for k in range(0, count, batch):
            rows = [grid_rows[pl.ds(index[offset + k + j], 1), :] for j in range(batch)]
            for j in range(batch):
                sticks[pl.ds(base + k + j, 1), :] = rows[j]

    walk(columns, index, index_sem, gather)

    def from_rows(i, _):
        first = sticks[pl.ds(i * 2 * LANES, LANES), :].T[:values]
        second = sticks[pl.ds(i * 2 * LANES + LANES, LANES), :].T[:values]
        block = jnp.concatenate([first, second], axis=0)
        depth = send.shape[2]
        for k in range(send.shape[1]):
            send[i, k] = block[k * depth : (k + 1) * depth]
        return 0

    lax.fori_loop(0, blocks, from_rows, 0, unroll=4)


def plane_call(recv, potential, columns, cosine, sine):
    freqs = cosine.shape[1]
    tables = plane_tables(cosine, sine)
    wide_v = tables[3].shape[1] // 2
    chunk = 1024
    vmem = pl.BlockSpec(memory_space=pltpu.VMEM)
    anywhere = pl.BlockSpec(memory_space=pl.ANY)
    along_v = columns % freqs
    along_u = columns // freqs
    along_u = along_u % 2 * (freqs // 2) + along_u // 2
    return pl.pallas_call(
        plane_kernel,
        out_shape=jax.ShapeDtypeStruct(recv.shape, jnp.float32),
        in_specs=[anywhere, vmem] + [anywhere] * 5,
        out_specs=vmem,
        scratch_shapes=[
            pltpu.VMEM((columns.shape[0], LANES), jnp.float32),
            pltpu.VMEM((freqs * freqs, LANES), jnp.float32),
            pltpu.VMEM((wide_v // LANES, freqs * ROWS, LANES), jnp.float32),
            pltpu.VMEM((wide_v // LANES, ROWS * freqs, LANES), jnp.float32),
            pltpu.VMEM(potential.shape, jnp.float32),
            *[pltpu.VMEM(table.shape, jnp.bfloat16) for table in tables],
            pltpu.SMEM((2 * chunk,), jnp.int32),
            pltpu.SemaphoreType.DMA((5,)),
            pltpu.SemaphoreType.DMA((2,)),
        ],
        compiler_params=pltpu.CompilerParams(vmem_limit_bytes=60 * 1024 * 1024),
        name="planes",
    )(along_u * freqs + along_v, recv, potential, *tables)


def greet(position, count):
    barrier = pltpu.get_barrier_semaphore()

    def signal(k, _):
        pl.semaphore_signal(barrier, inc=1, device_id={"fft": lax.rem(position + k, count)}, device_id_type=MESH)
        return 0

    lax.fori_loop(1, count, signal, 0)
    return barrier


def await_others(buffer, semaphore):
    others = buffer.at[pl.ds(0, buffer.shape[0] - 1)]
    pltpu.make_async_copy(others, others, semaphore).wait()


def start_loads(pairs, semaphore):
    loads = [pltpu.make_async_copy(source, target, semaphore.at[k]) for k, (source, target) in enumerate(pairs)]
    for load in loads:
        load.start()
    return loads


def spread_kernel(
    psi_hbm,
    high_hbm,
    low_hbm,
    recv,
    psi,
    table_high,
    table_low,
    staged,
    send,
    load_sem,
    send_sem,
    recv_sem,
):
    count, pieces, depth, _ = recv.shape
    values = pieces * depth // 2
    position = lax.axis_index("fft")
    loads = start_loads(((psi_hbm, psi), (high_hbm, table_high), (low_hbm, table_low)), load_sem)
    barrier = greet(position, count)
    for load in loads:
        load.wait()
    high, low = split(psi[...])
    staged[...] = dot(table_high[...], high) + dot(table_low[...], high) + dot(table_high[...], low)
    pl.semaphore_wait(barrier, count - 1)

    def stage(peer):
        rows = staged[pl.ds(peer * ROWS, ROWS), :]
        block = jnp.concatenate([rows[:values, :LANES], rows[:values, LANES:]], axis=0)
        return [block[k * depth : (k + 1) * depth] for k in range(pieces)]

    def post(k, _):
        peer = lax.rem(position + k, count)
        for at, piece in enumerate(stage(peer)):
            send[peer, at] = piece
        pltpu.make_async_remote_copy(
            src_ref=send.at[peer],
            dst_ref=recv.at[position],
            send_sem=send_sem,
            recv_sem=recv_sem,
            device_id={"fft": peer},
            device_id_type=MESH,
        ).start()
        return 0

    lax.fori_loop(1, count, post, 0)
    for at, piece in enumerate(stage(position)):
        recv[position, at] = piece
    await_others(recv, recv_sem)
    await_others(recv, send_sem)


def spread_call(psi, table, count, planes_held):
    rows = table.shape[0]
    vmem = pl.BlockSpec(memory_space=pltpu.VMEM)
    shape = (count, planes_held, 2 * psi.shape[1] // LANES, LANES)
    return pl.pallas_call(
        spread_kernel,
        out_shape=jax.ShapeDtypeStruct(shape, jnp.float32),
        in_specs=[pl.BlockSpec(memory_space=pl.ANY)] * 3,
        out_specs=vmem,
        scratch_shapes=[
            pltpu.VMEM(psi.shape, jnp.float32),
            pltpu.VMEM(table.shape, jnp.bfloat16),
            pltpu.VMEM(table.shape, jnp.bfloat16),
            pltpu.VMEM((rows, psi.shape[1]), jnp.float32),
            pltpu.VMEM(shape, jnp.float32),
            pltpu.SemaphoreType.DMA((3,)),
            pltpu.SemaphoreType.DMA,
            pltpu.SemaphoreType.DMA,
        ],
        compiler_params=pltpu.CompilerParams(
            collective_id=0, has_side_effects=True, vmem_limit_bytes=60 * 1024 * 1024
        ),
        name="spread",
    )(psi, *halves(table))


def collect_kernel(
    scale,
    weight,
    picked,
    columns,
    psi_hbm,
    *rest,
):
    bands = lax.axis_size("band")
    other_hbm, rest = rest[: bands - 1], rest[bands - 1 :]
    (
        high_hbm,
        low_hbm,
        hpsi,
        margin,
        psi,
        others,
        table_high,
        table_low,
        got,
        right,
        sums,
        load_sem,
        send_sem,
        recv_sem,
        sum_send_sem,
        sum_recv_sem,
    ) = rest
    count, pieces, depth, _ = picked.shape
    values = pieces * depth // 2
    freqs = hpsi.shape[2]
    position = lax.axis_index("fft")
    own = lax.axis_index("band")
    pairs = [(psi_hbm, psi), (high_hbm, table_high), (low_hbm, table_low)]
    pairs += [(source, others.at[k]) for k, source in enumerate(other_hbm)]
    loads = start_loads(pairs, load_sem)
    barrier = greet(position, count)
    pl.semaphore_wait(barrier, count - 1)

    def post(k, _):
        peer = lax.rem(position + k, count)
        pltpu.make_async_remote_copy(
            src_ref=picked.at[peer],
            dst_ref=got.at[position],
            send_sem=send_sem,
            recv_sem=recv_sem,
            device_id={"fft": peer},
            device_id_type=MESH,
        ).start()
        return 0

    lax.fori_loop(1, count, post, 0)
    got[position] = picked[position]
    for load in loads:
        load.wait()
    mine = columns[pl.ds(position * 2, 2), :]
    mine = jnp.concatenate([mine[0:1], mine[1:2]], axis=1)
    centre = freqs // 2
    along_u = jnp.floor((mine.astype(jnp.float32) + 0.5) * (1.0 / freqs)).astype(jnp.int32)
    along_v = mine - along_u * freqs - centre
    along_u = along_u - centre
    along_w = lax.broadcasted_iota(jnp.int32, (freqs, mine.shape[1]), 0) - centre
    squared = along_w * along_w + (along_u * along_u + along_v * along_v)
    kinetic = squared.astype(jnp.float32) * (0.5 / float(centre * centre))
    await_others(got, recv_sem)

    def to_right(i, _):
        block = jnp.concatenate([got[i, k] for k in range(pieces)], axis=0)
        blank = jnp.zeros((ROWS - values, LANES), jnp.float32)
        at = pl.multiple_of(i * ROWS, ROWS)
        right[pl.ds(at, ROWS), 0:LANES] = jnp.concatenate([block[:values], blank], axis=0)
        right[pl.ds(at, ROWS), LANES : 2 * LANES] = jnp.concatenate([block[values:], blank], axis=0)
        return 0

    lax.fori_loop(0, count, to_right, 0, unroll=4)
    high, low = split(right[...])
    applied = dot(table_high[...], high) + dot(table_low[...], high) + dot(table_high[...], low)
    right_re = kinetic * psi[0:freqs, :] + applied[:freqs] * scale
    right_im = kinetic * psi[freqs : 2 * freqs, :] + applied[freqs:] * scale
    hpsi[0, 0] = right_re
    hpsi[1, 0] = right_im

    def folded(product):
        narrow = product[:, :LANES] + product[:, LANES:]
        return jnp.sum(narrow, axis=0, keepdims=True)

    line = lax.broadcasted_iota(jnp.int32, (2 * bands, LANES), 0)
    tile = jnp.zeros((2 * bands, LANES), jnp.float32)
    for k in range(bands):
        left = psi if k == 0 else others.at[k - 1]
        left_re, left_im = left[0:freqs, :], left[freqs : 2 * freqs, :]
        row = lax.rem(own + k, bands)
        tile = jnp.where(line == row, folded(left_re * right_re + left_im * right_im), tile)
        tile = jnp.where(line == row + bands, folded(left_re * right_im - left_im * right_re), tile)
    sums[position] = tile * weight

    def post_sums(k, _):
        pltpu.make_async_remote_copy(
            src_ref=sums.at[position],
            dst_ref=sums.at[position],
            send_sem=sum_send_sem,
            recv_sem=sum_recv_sem,
            device_id={"fft": lax.rem(position + k, count)},
            device_id_type=MESH,
        ).start()
        return 0

    lax.fori_loop(1, count, post_sums, 0)
    await_others(sums, sum_recv_sem)
    margin[...] = jnp.sum(jnp.sum(sums[...], axis=0), axis=1, keepdims=True)
    await_others(got, send_sem)
    await_others(sums, sum_send_sem)


def collect_call(picked, columns, psi, others, table, scale, weight, shape):
    count = picked.shape[0]
    vmem = pl.BlockSpec(memory_space=pltpu.VMEM)
    anywhere = pl.BlockSpec(memory_space=pl.ANY)
    height = 2 * (len(others) + 1)
    table = table.T
    return pl.pallas_call(
        functools.partial(collect_kernel, scale, weight),
        out_shape=(jax.ShapeDtypeStruct(shape, jnp.float32), jax.ShapeDtypeStruct((height, 1), jnp.float32)),
        in_specs=[vmem] * 2 + [anywhere] * (3 + len(others)),
        out_specs=(vmem, vmem),
        scratch_shapes=[
            pltpu.VMEM(psi.shape, jnp.float32),
            pltpu.VMEM((len(others), *psi.shape), jnp.float32),
            pltpu.VMEM(table.shape, jnp.bfloat16),
            pltpu.VMEM(table.shape, jnp.bfloat16),
            pltpu.VMEM(picked.shape, jnp.float32),
            pltpu.VMEM((count * ROWS, psi.shape[1]), jnp.float32),
            pltpu.VMEM((count, height, LANES), jnp.float32),
            pltpu.SemaphoreType.DMA((3 + len(others),)),
            pltpu.SemaphoreType.DMA,
            pltpu.SemaphoreType.DMA,
            pltpu.SemaphoreType.DMA,
            pltpu.SemaphoreType.DMA,
        ],
        compiler_params=pltpu.CompilerParams(
            collective_id=1, has_side_effects=True, vmem_limit_bytes=60 * 1024 * 1024
        ),
        name="collect",
    )(picked, columns.reshape(-1, LANES), psi, *others, *halves(table))


def on_device(psi, potential, stick_columns):
    freq_count = psi.shape[2]
    per_device = psi.shape[3]
    grid_size = potential.shape[1]
    plane_count = potential.shape[0]
    fft_count = lax.axis_size("fft")
    cosine, sine = dft_tables(grid_size, freq_count)
    table = np.stack([np.concatenate([cosine, -sine], 1), np.concatenate([sine, cosine], 1)])
    table = table.reshape(2, fft_count, plane_count, 2 * freq_count).transpose(1, 0, 2, 3)
    table = table.reshape(fft_count, 2 * plane_count, 2 * freq_count)
    table = np.pad(table, ((0, 0), (0, ROWS - 2 * plane_count), (0, 0))).reshape(fft_count * ROWS, 2 * freq_count)
    flat_psi = psi.reshape(2 * freq_count, per_device)
    moved = spread_call(flat_psi, table, fft_count, plane_count)
    bands = lax.axis_size("band")
    held, moved = lax.optimization_barrier((flat_psi, moved))
    others = [
        lax.ppermute(held, "band", [((i + k) % bands, i) for i in range(bands)]) for k in range(1, bands)
    ]
    picked = plane_call(moved, potential, stick_columns, cosine, sine)
    scale = 1.0 / float(grid_size * grid_size * grid_size)
    weight = 1.0 / float(freq_count * per_device * fft_count)
    hpsi, margin = collect_call(picked, stick_columns, flat_psi, others, table, scale, weight, psi.shape)
    return (hpsi, margin.reshape(2, bands, 1))


def solution(mesh):
    placed = (P(None, "band", None, "fft"), P("fft", None, None), P())
    return jax.shard_map(
        on_device,
        mesh=mesh,
        in_specs=placed,
        out_specs=(P(None, "band", None, "fft"), P(None, None, "band")),
        check_vma=False,
    )
```

time: 141 us -> 114 us (0.81)
  the two profiles are of different devices: /device:TPU:225 before, /device:TPU:1 now
where the time goes in v2:
time: 114 us; the launch traced here: 113 us
  Pallas kernels  97.3 us (85%)
  starting transfers between devices  10.2 us (9%)
  local copies, waits for them, and re-layouts  3.27 us (3%)
  other arithmetic  1.55 us (1%)
    pallas_call x1, Pallas kernels, plane_call(): pl.pallas_call(plane_kernel, out_shape=jax.ShapeDtypeStruct(recv.shape, j...  52.2 us
    pallas_call x1, Pallas kernels, collect_call(): pl.pallas_call(functools.partial(collect_kernel, scale, weight), out_shap...  25.7 us
    pallas_call x1, Pallas kernels, spread_call(): pl.pallas_call(spread_kernel, out_shape=jax.ShapeDtypeStruct(shape, jnp.f...  19.4 us
    ppermute x3, starting transfers between devices, on_device(): lax.ppermute(held, 'band', [((i + k) % bands, i) for i in range(bands)])  10.2 us
    unnamed x11, local copies, waits for them, and re-layouts  2.62 us
  transfers between devices with their start and end apart: 3, of which 0 were waited for; matrix products, arithmetic and copies ran while one was open for 1% of the time, Pallas kernels for 46%

profile of v2, /device:TPU:1, one launch (start us, length us, event | category | flops | bytes accessed | tf_op | source)
XLA Modules:
  0.0 113.1 jit_solution(16017482832206199291)
XLA Ops:
  0.6 0.0 copy-start
  0.6 0.0 copy-start.4
  0.7 19.4 %spread.1.recv = f32[64,5,4,128]{3,2,1,0:T(4,128)} custom-call(f32[320,256]{1,0:T(8,128)} %bitcast.3, bf16[1024,320]{1,0:T(8,128)(2,1)} %constant.57.clone.high_hbm, bf16[1024,320]{1,0:T(8,128)(2,1)} %constant.58.clone.low_hbm), custom_call_target="tpu_custom_call" | custom-call | tf_op jit(solution)/shard_map/spread/pallas_call | solution.py:383
  20.0 0.0 copy-done
  20.1 3.1 %collective-permute-start.2 = (f32[320,256]{1,0:T(8,128)S(1)}, f32[320,256]{1,0:T(8,128)S(1)}, u32[]{:S(2)}, u32[]{:S(2)}) collective-permute-start(f32[320,256]{1,0:T(8,128)S(1)} %bitcast.5), channel_id=1, source_target_pairs={{192,0},{0,64},{64,128},{128,192},{193,1},{1,65},{65,129},{129,193... | collective-permute-start | bytes 983048 | tf_op jit(solution)/shard_map/ppermute | solution.py:567
  23.1 4.8 %collective-permute-start.1 = (f32[320,256]{1,0:T(8,128)S(1)}, f32[320,256]{1,0:T(8,128)S(1)}, u32[]{:S(2)}, u32[]{:S(2)}) collective-permute-start(f32[320,256]{1,0:T(8,128)S(1)} %bitcast.6), channel_id=1, source_target_pairs={{128,0},{192,64},{0,128},{64,192},{129,1},{193,65},{1,129},{65,193... | collective-permute-start | bytes 983048 | tf_op jit(solution)/shard_map/ppermute | solution.py:567
  27.9 2.4 %collective-permute-start = (f32[320,256]{1,0:T(8,128)S(1)}, f32[320,256]{1,0:T(8,128)S(1)}, u32[]{:S(2)}, u32[]{:S(2)}) collective-permute-start(f32[320,256]{1,0:T(8,128)S(1)} %bitcast.7), channel_id=1, source_target_pairs={{64,0},{128,64},{192,128},{0,192},{65,1},{129,65},{193,129},{1,193... | collective-permute-start | bytes 983048 | tf_op jit(solution)/shard_map/ppermute | solution.py:567
  30.3 0.0 copy-done.4
  30.3 0.8 fusion.3.columns
  31.0 52.2 %planes.1.picked = f32[64,5,4,128]{3,2,1,0:T(4,128)} custom-call(s32[16384]{0:T(1024)} %fusion.3.columns, f32[64,5,4,128]{3,2,1,0:T(4,128)} %spread.1.recv, f32[5,320,320]{2,1,0:T(8,128)} %potential_hbm.1, bf16[512,768]{1,0:T(8,128)(2,1)} %constant.59.clone.y_out_hbm, bf16[2,320,240]{2,1,0:T(8,128)(2,1)} %constant.60.clone.x_out_hbm, ...), custom_call_target="tpu_custom_call" | custom-call | tf_op jit(solution)/shard_map/planes/pallas_call | solution.py:284
  83.3 0.0 collective-permute-done.2.rest_2_
  83.3 0.0 copy-start.1
  83.3 0.0 collective-permute-done.1.rest_1_
  83.3 0.0 copy-start.2
  83.3 0.0 collective-permute-done.rest_0_
  83.3 0.0 copy-start.3
  83.3 0.7 copy-done.1
  84.0 0.1 copy-done.2
  84.2 0.1 copy-done.3
  84.2 25.7 %collect.1 = (f32[2,1,160,256]{3,2,1,0:T(8,128)}, f32[8,1]{1,0:T(8,128)}) custom-call(f32[64,5,4,128]{3,2,1,0:T(4,128)} %planes.1.picked, s32[128,128]{1,0:T(8,128)} %bitcast.8, f32[320,256]{1,0:T(8,128)} %bitcast.4, f32[320,256]{1,0:T(8,128)} %copy-done.3, f32[320,256]{1,0:T(8,128)} %copy-done.2, f32[320,256]{1,0:T(8,128)} %copy-done.1, ...), custom_call_target="tpu_custom_call" | custom-call | tf_op jit(solution)/shard_map/collect/pallas_call | solution.py:525
  109.9 0.8 reduce
  110.7 0.6 reshape.15
  111.4 1.7 %copy.16 = f32[2,1,160,256]{3,2,1,0:T(8,128)} copy(f32[2,1,160,256]{3,2,1,0:T(8,128)} %get-tuple-element.16) | data formatting | bytes 655360
Async XLA Ops:
  0.6 19.4 %copy-start = (f32[2,1,160,256]{3,2,1,0:T(8,128)S(1)}, f32[2,1,160,256]{3,2,1,0:T(8,128)}, u32[]{:S(2)}) copy-start(f32[2,1,160,256]{3,2,1,0:T(8,128)} %param.11) | copy-start | bytes 983044
  0.6 29.6 %copy-start.4 = (s32[16384]{0:T(1024)S(1)}, s32[16384]{0:T(1024)}, u32[]{:S(2)}) copy-start(s32[16384]{0:T(1024)} %param.13) | copy-start | bytes 196612
  20.1 63.2 %collective-permute-start.2 = (f32[320,256]{1,0:T(8,128)S(1)}, f32[320,256]{1,0:T(8,128)S(1)}, u32[]{:S(2)}, u32[]{:S(2)}) collective-permute-start(f32[320,256]{1,0:T(8,128)S(1)} %bitcast.5), channel_id=1, source_target_pairs={{192,0},{0,64},{64,128},{128,192},{193,1},{1,65},{65,129},{129,193... | collective-permute-start | bytes 983048 | tf_op jit(solution)/shard_map/ppermute | solution.py:567
  23.1 60.2 %collective-permute-start.1 = (f32[320,256]{1,0:T(8,128)S(1)}, f32[320,256]{1,0:T(8,128)S(1)}, u32[]{:S(2)}, u32[]{:S(2)}) collective-permute-start(f32[320,256]{1,0:T(8,128)S(1)} %bitcast.6), channel_id=1, source_target_pairs={{128,0},{192,64},{0,128},{64,192},{129,1},{193,65},{1,129},{65,193... | collective-permute-start | bytes 983048 | tf_op jit(solution)/shard_map/ppermute | solution.py:567
  27.9 55.4 %collective-permute-start = (f32[320,256]{1,0:T(8,128)S(1)}, f32[320,256]{1,0:T(8,128)S(1)}, u32[]{:S(2)}, u32[]{:S(2)}) collective-permute-start(f32[320,256]{1,0:T(8,128)S(1)} %bitcast.7), channel_id=1, source_target_pairs={{64,0},{128,64},{192,128},{0,192},{65,1},{129,65},{193,129},{1,193... | collective-permute-start | bytes 983048 | tf_op jit(solution)/shard_map/ppermute | solution.py:567
  83.3 0.7 copy-start.1
  83.3 0.8 copy-start.2
  83.3 0.9 copy-start.3

commit v3 on v2

--- a/solution.py
+++ b/solution.py
@@ -101,11 +101,12 @@
     return real, imag
 
 
-def walk(columns, index, index_sem, visit):
+def walk(columns, index, index_sem, visit, first=0):
     chunk = index.shape[0] // 2
     pairs = columns.shape[0] // (2 * chunk)
 
-    def fetch(number, slot):
+    def fetch(step, slot):
+        number = lax.rem(first + step, 2 * pairs)
         source = columns.at[pl.ds(pl.multiple_of(number * chunk, chunk), chunk)]
         return pltpu.make_async_copy(source, index.at[pl.ds(slot * chunk, chunk)], index_sem.at[slot])
 
@@ -114,97 +115,26 @@
     def pair(i, _):
         fetch(2 * i + 1, 1).start()
         fetch(2 * i, 0).wait()
-        visit(2 * i * chunk, 0, chunk)
+        visit(lax.rem(first + 2 * i, 2 * pairs), 0, chunk)
 
         @pl.when(i < pairs - 1)
         def _():
             fetch(2 * i + 2, 0).start()
 
         fetch(2 * i + 1, 1).wait()
-        visit(2 * i * chunk + chunk, chunk, chunk)
+        visit(lax.rem(first + 2 * i + 1, 2 * pairs), chunk, chunk)
         return 0
 
     lax.fori_loop(0, pairs, pair, 0)
 
 
-def plane_kernel(
-    columns,
-    recv,
-    potential_hbm,
-    y_out_hbm,
-    x_out_hbm,
-    x_back_hbm,
-    y_back_hbm,
-    send,
-    sticks,
-    grid_rows,
-    flat,
-    planes,
-    potential,
-    y_out,
-    x_out,
-    x_back,
-    y_back,
-    index,
-    load_sem,
-    index_sem,
-):
+def through_planes(flat, planes, potential, y_out, x_out, x_back, y_back):
     planes_held, grid, _ = potential.shape
     half = grid // 2
     freqs = x_back.shape[1]
     even = freqs // 2
     wide = y_out.shape[1] // 2
     wide_v = y_back.shape[1] // 2
-    blocks = recv.shape[0]
-    values = 2 * planes_held
-    batch = 64
-
-    loads = start_loads(
-        (
-            (potential_hbm, potential),
-            (y_out_hbm, y_out),
-            (x_out_hbm, x_out),
-            (x_back_hbm, x_back),
-            (y_back_hbm, y_back),
-        ),
-        load_sem,
-    )
-
-    def clear(i, _):
-        grid_rows[pl.ds(i * freqs, freqs), :] = jnp.zeros((freqs, LANES), jnp.float32)
-        return 0
-
-    lax.fori_loop(0, freqs, clear, 0)
-
-    def to_rows(i, _):
-        block = jnp.concatenate([recv[i, k] for k in range(recv.shape[1])], axis=0)
-        block = jnp.concatenate([block, jnp.zeros((LANES - block.shape[0], LANES), jnp.float32)], axis=0)
-        turned = block.T
-        sticks[pl.ds(i * 2 * LANES, LANES), :] = turned
-        sticks[pl.ds(i * 2 * LANES + LANES, LANES), :] = pltpu.roll(turned, LANES - values, 1)
-        return 0
-
-    lax.fori_loop(0, blocks, to_rows, 0, unroll=4)
-
-    def scatter(base, offset, count):
-        base = pl.multiple_of(base, count)
-        for k in range(0, count, batch):
-            rows = [sticks[pl.ds(base + k + j, 1), :] for j in range(batch)]
-            for j in range(batch):
-                grid_rows[pl.ds(index[offset + k + j], 1), :] = rows[j]
-
-    walk(columns, index, index_sem, scatter)
-
-    def to_planes(u, _):
-        turned = grid_rows[pl.ds(u * freqs, freqs), :].T
-        for k in range(flat.shape[0]):
-            upper = min(freqs - k * LANES, LANES)
-            flat[k, pl.ds(u * ROWS, ROWS), 0:upper] = turned[0:ROWS, k * LANES : k * LANES + upper]
-        return 0
-
-    lax.fori_loop(0, freqs, to_planes, 0, unroll=8)
-    for load in loads:
-        load.wait()
 
     def plane(z, _):
         lane = lax.broadcasted_iota(jnp.int32, (2 * freqs, LANES), 1)
@@ -241,88 +171,92 @@
 
     lax.fori_loop(0, planes_held, plane, 0)
 
-    def from_planes(u, _):
-        for k in range(planes.shape[0]):
-            upper = min(freqs - k * LANES, LANES)
-            turned = planes[k, pl.ds(u, ROWS, stride=freqs), :].T
-            grid_rows[pl.ds(u * freqs + k * LANES, upper), 0:ROWS] = turned[:upper]
-        return 0
-
-    lax.fori_loop(0, freqs, from_planes, 0, unroll=8)
-
-    def gather(base, offset, count):
-        base = pl.multiple_of(base, count)
-        for k in range(0, count, batch):
-            rows = [grid_rows[pl.ds(index[offset + k + j], 1), :] for j in range(batch)]
-            for j in range(batch):
-                sticks[pl.ds(base + k + j, 1), :] = rows[j]
-
-    walk(columns, index, index_sem, gather)
-
-    def from_rows(i, _):
-        first = sticks[pl.ds(i * 2 * LANES, LANES), :].T[:values]
-        second = sticks[pl.ds(i * 2 * LANES + LANES, LANES), :].T[:values]
-        block = jnp.concatenate([first, second], axis=0)
-        depth = send.shape[2]
-        for k in range(send.shape[1]):
-            send[i, k] = block[k * depth : (k + 1) * depth]
-        return 0
-
-    lax.fori_loop(0, blocks, from_rows, 0, unroll=4)
-
-
-def plane_call(recv, potential, columns, cosine, sine):
-    freqs = cosine.shape[1]
-    tables = plane_tables(cosine, sine)
-    wide_v = tables[3].shape[1] // 2
-    chunk = 1024
-    vmem = pl.BlockSpec(memory_space=pltpu.VMEM)
-    anywhere = pl.BlockSpec(memory_space=pl.ANY)
-    along_v = columns % freqs
-    along_u = columns // freqs
-    along_u = along_u % 2 * (freqs // 2) + along_u // 2
-    return pl.pallas_call(
-        plane_kernel,
-        out_shape=jax.ShapeDtypeStruct(recv.shape, jnp.float32),
-        in_specs=[anywhere, vmem] + [anywhere] * 5,
-        out_specs=vmem,
-        scratch_shapes=[
-            pltpu.VMEM((columns.shape[0], LANES), jnp.float32),
-            pltpu.VMEM((freqs * freqs, LANES), jnp.float32),
-            pltpu.VMEM((wide_v // LANES, freqs * ROWS, LANES), jnp.float32),
-            pltpu.VMEM((wide_v // LANES, ROWS * freqs, LANES), jnp.float32),
-            pltpu.VMEM(potential.shape, jnp.float32),
-            *[pltpu.VMEM(table.shape, jnp.bfloat16) for table in tables],
-            pltpu.SMEM((2 * chunk,), jnp.int32),
-            pltpu.SemaphoreType.DMA((5,)),
-            pltpu.SemaphoreType.DMA((2,)),
-        ],
-        compiler_params=pltpu.CompilerParams(vmem_limit_bytes=60 * 1024 * 1024),
-        name="planes",
-    )(along_u * freqs + along_v, recv, potential, *tables)
-
-
-def greet(position, count):
-    barrier = pltpu.get_barrier_semaphore()
-
-    def signal(k, _):
-        pl.semaphore_signal(barrier, inc=1, device_id={"fft": lax.rem(position + k, count)}, device_id_type=MESH)
-        return 0
-
-    lax.fori_loop(1, count, signal, 0)
-    return barrier
-
-
-def await_others(buffer, semaphore):
-    others = buffer.at[pl.ds(0, buffer.shape[0] - 1)]
-    pltpu.make_async_copy(others, others, semaphore).wait()
-
 
 def start_loads(pairs, semaphore):
     loads = [pltpu.make_async_copy(source, target, semaphore.at[k]) for k, (source, target) in enumerate(pairs)]
     for load in loads:
         load.start()
     return loads
+
+
+def place_kernel(columns, recv, flat, sticks, grid_rows, index, index_sem):
+    blocks, pieces, depth, _ = recv.shape
+    values = pieces * depth // 2
+    freqs = flat.shape[1] // ROWS
+    batch = 64
+
+    def clear(i, _):
+        grid_rows[pl.ds(i * freqs, freqs), :] = jnp.zeros((freqs, LANES), jnp.float32)
+        return 0
+
+    lax.fori_loop(0, freqs, clear, 0)
+
+    def to_rows(i, _):
+        block = jnp.concatenate([recv[i, k] for k in range(pieces)], axis=0)
+        block = jnp.concatenate([block, jnp.zeros((LANES - block.shape[0], LANES), jnp.float32)], axis=0)
+        turned = block.T
+        sticks[pl.ds(i * 2 * LANES, LANES), :] = turned
+        sticks[pl.ds(i * 2 * LANES + LANES, LANES), :] = pltpu.roll(turned, LANES - values, 1)
+        return 0
+
+    lax.fori_loop(0, blocks, to_rows, 0, unroll=4)
+
+    def scatter(number, offset, count):
+        base = pl.multiple_of(number * count, count)
+        for k in range(0, count, batch):
+            rows = [sticks[pl.ds(base + k + j, 1), :] for j in range(batch)]
+            for j in range(batch):
+                grid_rows[pl.ds(index[offset + k + j], 1), :] = rows[j]
+
+    walk(columns, index, index_sem, scatter)
+
+    def to_planes(u, _):
+        turned = grid_rows[pl.ds(u * freqs, freqs), :].T
+        for k in range(flat.shape[0]):
+            upper = min(freqs - k * LANES, LANES)
+            flat[k, pl.ds(u * ROWS, ROWS), 0:upper] = turned[0:ROWS, k * LANES : k * LANES + upper]
+        return 0
+
+    lax.fori_loop(0, freqs, to_planes, 0, unroll=8)
+
+
+def place_call(recv, columns, freqs):
+    chunk = 1024
+    tiles = -(-freqs // LANES)
+    vmem = pl.BlockSpec(memory_space=pltpu.VMEM)
+    anywhere = pl.BlockSpec(memory_space=pl.ANY)
+    return pl.pallas_call(
+        place_kernel,
+        out_shape=jax.ShapeDtypeStruct((tiles, freqs * ROWS, LANES), jnp.float32),
+        in_specs=[anywhere, vmem],
+        out_specs=vmem,
+        scratch_shapes=[
+            pltpu.VMEM((columns.shape[0], LANES), jnp.float32),
+            pltpu.VMEM((freqs * freqs, LANES), jnp.float32),
+            pltpu.SMEM((2 * chunk,), jnp.int32),
+            pltpu.SemaphoreType.DMA((2,)),
+        ],
+        compiler_params=pltpu.CompilerParams(vmem_limit_bytes=60 * 1024 * 1024),
+        name="place",
+    )(columns, recv)
+
+
+def greet(position, count, own=None, bands=1):
+    barrier = pltpu.get_barrier_semaphore()
+    for k in range(1, bands):
+        pl.semaphore_signal(barrier, inc=1, device_id={"band": lax.rem(own + k, bands)}, device_id_type=MESH)
+
+    def signal(k, _):
+        pl.semaphore_signal(barrier, inc=1, device_id={"fft": lax.rem(position + k, count)}, device_id_type=MESH)
+        return 0
+
+    lax.fori_loop(1, count, signal, 0)
+    return barrier
+
+
+def await_others(buffer, semaphore):
+    others = buffer.at[pl.ds(0, buffer.shape[0] - 1)]
+    pltpu.make_async_copy(others, others, semaphore).wait()
 
 
 def spread_kernel(
@@ -405,58 +339,126 @@
 def collect_kernel(
     scale,
     weight,
-    picked,
+    index_hbm,
     columns,
     psi_hbm,
-    *rest,
+    flat_hbm,
+    potential_hbm,
+    high_hbm,
+    low_hbm,
+    y_out_hbm,
+    x_out_hbm,
+    x_back_hbm,
+    y_back_hbm,
+    hpsi,
+    margin,
+    psi,
+    flat,
+    potential,
+    table_high,
+    table_low,
+    y_out,
+    x_out,
+    x_back,
+    y_back,
+    others,
+    planes,
+    grid_rows,
+    sticks,
+    send,
+    got,
+    right,
+    sums,
+    index,
+    index_sem,
+    load_sem,
+    band_send_sem,
+    band_recv_sem,
+    send_sem,
+    recv_sem,
+    sum_send_sem,
+    sum_recv_sem,
 ):
-    bands = lax.axis_size("band")
-    other_hbm, rest = rest[: bands - 1], rest[bands - 1 :]
-    (
-        high_hbm,
-        low_hbm,
-        hpsi,
-        margin,
-        psi,
-        others,
-        table_high,
-        table_low,
-        got,
-        right,
-        sums,
-        load_sem,
-        send_sem,
-        recv_sem,
-        sum_send_sem,
-        sum_recv_sem,
-    ) = rest
-    count, pieces, depth, _ = picked.shape
+    bands = others.shape[0] + 1
+    count, pieces, depth, _ = got.shape
     values = pieces * depth // 2
     freqs = hpsi.shape[2]
+    per_device = hpsi.shape[3]
+    batch = 64
     position = lax.axis_index("fft")
     own = lax.axis_index("band")
-    pairs = [(psi_hbm, psi), (high_hbm, table_high), (low_hbm, table_low)]
-    pairs += [(source, others.at[k]) for k, source in enumerate(other_hbm)]
-    loads = start_loads(pairs, load_sem)
-    barrier = greet(position, count)
-    pl.semaphore_wait(barrier, count - 1)
-
-    def post(k, _):
-        peer = lax.rem(position + k, count)
+    loads = start_loads(
+        (
+            (flat_hbm, flat),
+            (y_out_hbm, y_out),
+            (x_out_hbm, x_out),
+            (potential_hbm, potential),
+            (x_back_hbm, x_back),
+            (y_back_hbm, y_back),
+            (psi_hbm, psi),
+            (high_hbm, table_high),
+            (low_hbm, table_low),
+        ),
+        load_sem,
+    )
+    barrier = greet(position, count, own, bands)
+    pl.semaphore_wait(barrier, count + bands - 2)
+    band_copies = [
         pltpu.make_async_remote_copy(
-            src_ref=picked.at[peer],
-            dst_ref=got.at[position],
-            send_sem=send_sem,
-            recv_sem=recv_sem,
-            device_id={"fft": peer},
+            src_ref=psi_hbm,
+            dst_ref=others.at[k - 1],
+            send_sem=band_send_sem.at[k - 1],
+            recv_sem=band_recv_sem.at[k - 1],
+            device_id={"band": lax.rem(own + bands - k, bands)},
             device_id_type=MESH,
-        ).start()
-        return 0
-
-    lax.fori_loop(1, count, post, 0)
-    got[position] = picked[position]
+        )
+        for k in range(1, bands)
+    ]
+    for copy in band_copies:
+        copy.start()
     for load in loads:
         load.wait()
+    through_planes(flat, planes, potential, y_out, x_out, x_back, y_back)
+
+    def from_planes(u, _):
+        for k in range(planes.shape[0]):
+            upper = min(freqs - k * LANES, LANES)
+            turned = planes[k, pl.ds(u, ROWS, stride=freqs), :].T
+            grid_rows[pl.ds(u * freqs + k * LANES, upper), 0:ROWS] = turned[:upper]
+        return 0
+
+    lax.fori_loop(0, freqs, from_planes, 0, unroll=8)
+
+    def gather(number, offset, length):
+        for k in range(0, length, batch):
+            rows = [grid_rows[pl.ds(index[offset + k + j], 1), :] for j in range(batch)]
+            for j in range(batch):
+                sticks[pl.ds(offset + k + j, 1), :] = rows[j]
+        group = length // per_device
+        for k in range(group):
+            at = offset + k * per_device
+            first = sticks[pl.ds(at, LANES), :].T[:values]
+            second = sticks[pl.ds(at + LANES, LANES), :].T[:values]
+            block = jnp.concatenate([first, second], axis=0)
+            for piece in range(pieces):
+                send[number * group + k, piece] = block[piece * depth : (piece + 1) * depth]
+        for k in range(group):
+            peer = number * group + k
+
+            @pl.when(peer != position)
+            def _(peer=peer):
+                pltpu.make_async_remote_copy(
+                    src_ref=send.at[peer],
+                    dst_ref=got.at[position],
+                    send_sem=send_sem,
+                    recv_sem=recv_sem,
+                    device_id={"fft": peer},
+                    device_id_type=MESH,
+                ).start()
+
+    chunk = index.shape[0] // 2
+    walk(index_hbm, index, index_sem, gather, lax.div(position * per_device, chunk) + 1)
+    got[position] = send[position]
     mine = columns[pl.ds(position * 2, 2), :]
     mine = jnp.concatenate([mine[0:1], mine[1:2]], axis=1)
     centre = freqs // 2
@@ -488,6 +490,8 @@
         narrow = product[:, :LANES] + product[:, LANES:]
         return jnp.sum(narrow, axis=0, keepdims=True)
 
+    for copy in band_copies:
+        copy.wait()
     line = lax.broadcasted_iota(jnp.int32, (2 * bands, LANES), 0)
     tile = jnp.zeros((2 * bands, LANES), jnp.float32)
     for k in range(bands):
@@ -516,26 +520,36 @@
     await_others(sums, sum_send_sem)
 
 
-def collect_call(picked, columns, psi, others, table, scale, weight, shape):
-    count = picked.shape[0]
+def collect_call(flat, potential, renumbered, columns, psi, table, cosine, sine, scale, weight, shape, count, bands):
+    freqs = cosine.shape[1]
+    planes_held = potential.shape[0]
     vmem = pl.BlockSpec(memory_space=pltpu.VMEM)
     anywhere = pl.BlockSpec(memory_space=pl.ANY)
-    height = 2 * (len(others) + 1)
+    chunk = 1024
     table = table.T
+    tables = plane_tables(cosine, sine)
+    blocks = (count, planes_held, 2 * psi.shape[1] // LANES, LANES)
+    operands = (psi, flat, potential, *halves(table), *tables)
     return pl.pallas_call(
         functools.partial(collect_kernel, scale, weight),
-        out_shape=(jax.ShapeDtypeStruct(shape, jnp.float32), jax.ShapeDtypeStruct((height, 1), jnp.float32)),
-        in_specs=[vmem] * 2 + [anywhere] * (3 + len(others)),
+        out_shape=(jax.ShapeDtypeStruct(shape, jnp.float32), jax.ShapeDtypeStruct((2 * bands, 1), jnp.float32)),
+        in_specs=[anywhere, vmem] + [anywhere] * len(operands),
         out_specs=(vmem, vmem),
         scratch_shapes=[
-            pltpu.VMEM(psi.shape, jnp.float32),
-            pltpu.VMEM((len(others), *psi.shape), jnp.float32),
-            pltpu.VMEM(table.shape, jnp.bfloat16),
-            pltpu.VMEM(table.shape, jnp.bfloat16),
-            pltpu.VMEM(picked.shape, jnp.float32),
+            *[pltpu.VMEM(operand.shape, operand.dtype) for operand in operands],
+            pltpu.VMEM((bands - 1, *psi.shape), jnp.float32),
+            pltpu.VMEM((flat.shape[0], ROWS * freqs, LANES), jnp.float32),
+            pltpu.VMEM((freqs * freqs, LANES), jnp.float32),
+            pltpu.VMEM((2 * chunk, LANES), jnp.float32),
+            pltpu.VMEM(blocks, jnp.float32),
+            pltpu.VMEM(blocks, jnp.float32),
             pltpu.VMEM((count * ROWS, psi.shape[1]), jnp.float32),
-            pltpu.VMEM((count, height, LANES), jnp.float32),
-            pltpu.SemaphoreType.DMA((3 + len(others),)),
+            pltpu.VMEM((count, 2 * bands, LANES), jnp.float32),
+            pltpu.SMEM((2 * chunk,), jnp.int32),
+            pltpu.SemaphoreType.DMA((2,)),
+            pltpu.SemaphoreType.DMA((len(operands),)),
+            pltpu.SemaphoreType.DMA((bands - 1,)),
+            pltpu.SemaphoreType.DMA((bands - 1,)),
             pltpu.SemaphoreType.DMA,
             pltpu.SemaphoreType.DMA,
             pltpu.SemaphoreType.DMA,
@@ -545,7 +559,7 @@
             collective_id=1, has_side_effects=True, vmem_limit_bytes=60 * 1024 * 1024
         ),
         name="collect",
-    )(picked, columns.reshape(-1, LANES), psi, *others, *halves(table))
+    )(renumbered, columns.reshape(-1, LANES), *operands)
 
 
 def on_device(psi, potential, stick_columns):
@@ -562,14 +576,28 @@
     flat_psi = psi.reshape(2 * freq_count, per_device)
     moved = spread_call(flat_psi, table, fft_count, plane_count)
     bands = lax.axis_size("band")
-    held, moved = lax.optimization_barrier((flat_psi, moved))
-    others = [
-        lax.ppermute(held, "band", [((i + k) % bands, i) for i in range(bands)]) for k in range(1, bands)
-    ]
-    picked = plane_call(moved, potential, stick_columns, cosine, sine)
+    along_v = stick_columns % freq_count
+    along_u = stick_columns // freq_count
+    along_u = along_u % 2 * (freq_count // 2) + along_u // 2
+    renumbered = along_u * freq_count + along_v
+    flat = place_call(moved, renumbered, freq_count)
     scale = 1.0 / float(grid_size * grid_size * grid_size)
     weight = 1.0 / float(freq_count * per_device * fft_count)
-    hpsi, margin = collect_call(picked, stick_columns, flat_psi, others, table, scale, weight, psi.shape)
+    hpsi, margin = collect_call(
+        flat,
+        potential,
+        renumbered,
+        stick_columns,
+        flat_psi,
+        table,
+        cosine,
+        sine,
+        scale,
+        weight,
+        psi.shape,
+        fft_count,
+        bands,
+    )
     return (hpsi, margin.reshape(2, bands, 1))
 
 

time: 114 us -> 103 us (0.904)
  starting transfers between devices: 10.2 us -> 0 us
    pallas_call x1, Pallas kernels: 52.2 us -> 22.6 us  [place_call(): pl.pallas_call(place_kernel, out_shape=jax.ShapeDtypeStruct((tiles, freqs...]
    pallas_call x1, Pallas kernels: 25.7 us -> 55.2 us  [collect_call(): pl.pallas_call(functools.partial(collect_kernel, scale, weight), out_shap...]
    ppermute x3 -> x0, starting transfers between devices: 10.2 us -> none  [on_device(): lax.ppermute(held, 'band', [((i + k) % bands, i) for i in range(bands)])]
    unnamed x11 -> x1, local copies, waits for them, and re-layouts: 2.62 us -> 1.72 us
  transfers between devices with their start and end apart: 3 -> 0, of which waited for: 0 -> 0; matrix products, arithmetic and copies ran while one was open for 1% -> 0% of each run, Pallas kernels for 46% -> 0%
where the time goes in v3:
time: 103 us; the launch traced here: 102 us
  Pallas kernels  96.8 us (94%)
  other arithmetic  2.39 us (2%)
  local copies, waits for them, and re-layouts  2.36 us (2%)
    pallas_call x1, Pallas kernels, collect_call(): pl.pallas_call(functools.partial(collect_kernel, scale, weight), out_shap...  55.2 us
    pallas_call x1, Pallas kernels, place_call(): pl.pallas_call(place_kernel, out_shape=jax.ShapeDtypeStruct((tiles, freqs...  22.6 us
    pallas_call x1, Pallas kernels, spread_call(): pl.pallas_call(spread_kernel, out_shape=jax.ShapeDtypeStruct(shape, jnp.f...  19.1 us

profile of v3, /device:TPU:1, one launch (start us, length us, event | category | flops | bytes accessed | tf_op | source)
XLA Modules:
  0.0 102.2 jit_solution(8742692820433323286)
XLA Ops:
  0.6 1.6 %fusion.3.columns.index_hbm = s32[16384]{0:T(1024)} fusion(s32[16384]{0:T(1024)} %param.13), kind=kLoop, calls=%fused_computation.10 | loop fusion | flops 573440 | bytes 131072 | tf_op jit(solution)/shard_map/add | solution.py:582
  2.2 19.1 %spread.1.recv = f32[64,5,4,128]{3,2,1,0:T(4,128)} custom-call(f32[320,256]{1,0:T(8,128)} %bitcast.3, bf16[1024,320]{1,0:T(8,128)(2,1)} %constant.57.clone.high_hbm, bf16[1024,320]{1,0:T(8,128)(2,1)} %constant.58.clone.low_hbm), custom_call_target="tpu_custom_call" | custom-call | tf_op jit(solution)/shard_map/spread/pallas_call | solution.py:317
  21.3 22.6 %place.1.flat_hbm = f32[2,2560,128]{2,1,0:T(8,128)} custom-call(s32[16384]{0:T(1024)} %fusion.3.columns.index_hbm, f32[64,5,4,128]{3,2,1,0:T(4,128)} %spread.1.recv), custom_call_target="tpu_custom_call" | custom-call | tf_op jit(solution)/shard_map/place/pallas_call | solution.py:228
  43.9 55.2 %collect.1 = (f32[2,1,160,256]{3,2,1,0:T(8,128)}, f32[8,1]{1,0:T(8,128)}) custom-call(s32[16384]{0:T(1024)} %fusion.3.columns.index_hbm, s32[128,128]{1,0:T(8,128)} %bitcast.5, f32[320,256]{1,0:T(8,128)} %bitcast.4, f32[2,2560,128]{2,1,0:T(8,128)} %place.1.flat_hbm, f32[5,320,320]{2,1,0:T(8,128)} %potential_hbm.1, ...), custom_call_target="tpu_custom_call" | custom-call | tf_op jit(solution)/shard_map/collect/pallas_call | solution.py:533
  99.0 0.8 reduce
  99.8 0.6 reshape.15
  100.5 1.7 %copy.16 = f32[2,1,160,256]{3,2,1,0:T(8,128)} copy(f32[2,1,160,256]{3,2,1,0:T(8,128)} %get-tuple-element.12) | data formatting | bytes 655360

commit v4 on v3

--- a/solution.py
+++ b/solution.py
@@ -11,6 +11,8 @@
 
 LANES = 128
 ROWS = 16
+PACK = 4
+CHUNK = 1024
 MESH = pl.DeviceIdType.MESH
 
 
@@ -102,30 +104,31 @@
 
 
 def walk(columns, index, index_sem, visit, first=0):
-    chunk = index.shape[0] // 2
-    pairs = columns.shape[0] // (2 * chunk)
+    steps = columns.shape[0] // CHUNK
+
+    def number_of(step):
+        return lax.rem(first + step, steps)
 
     def fetch(step, slot):
-        number = lax.rem(first + step, 2 * pairs)
-        source = columns.at[pl.ds(pl.multiple_of(number * chunk, chunk), chunk)]
-        return pltpu.make_async_copy(source, index.at[pl.ds(slot * chunk, chunk)], index_sem.at[slot])
+        source = columns.at[pl.ds(pl.multiple_of(number_of(step) * CHUNK, CHUNK), CHUNK)]
+        return pltpu.make_async_copy(source, index.at[pl.ds(slot * CHUNK, CHUNK)], index_sem.at[slot])
 
     fetch(0, 0).start()
 
     def pair(i, _):
         fetch(2 * i + 1, 1).start()
         fetch(2 * i, 0).wait()
-        visit(lax.rem(first + 2 * i, 2 * pairs), 0, chunk)
-
-        @pl.when(i < pairs - 1)
+        visit(2 * i, 0)
+
+        @pl.when(i < steps // 2 - 1)
         def _():
             fetch(2 * i + 2, 0).start()
 
         fetch(2 * i + 1, 1).wait()
-        visit(lax.rem(first + 2 * i + 1, 2 * pairs), chunk, chunk)
-        return 0
-
-    lax.fori_loop(0, pairs, pair, 0)
+        visit(2 * i + 1, 1)
+        return 0
+
+    lax.fori_loop(0, steps // 2, pair, 0)
 
 
 def through_planes(flat, planes, potential, y_out, x_out, x_back, y_back):
@@ -179,7 +182,7 @@
     return loads
 
 
-def place_kernel(columns, recv, flat, sticks, grid_rows, index, index_sem):
+def place_kernel(index_hbm, columns, recv, flat, kinetic, sticks, grid_rows, index, index_sem):
     blocks, pieces, depth, _ = recv.shape
     values = pieces * depth // 2
     freqs = flat.shape[1] // ROWS
@@ -191,24 +194,30 @@
 
     lax.fori_loop(0, freqs, clear, 0)
 
-    def to_rows(i, _):
-        block = jnp.concatenate([recv[i, k] for k in range(pieces)], axis=0)
-        block = jnp.concatenate([block, jnp.zeros((LANES - block.shape[0], LANES), jnp.float32)], axis=0)
-        turned = block.T
-        sticks[pl.ds(i * 2 * LANES, LANES), :] = turned
-        sticks[pl.ds(i * 2 * LANES + LANES, LANES), :] = pltpu.roll(turned, LANES - values, 1)
-        return 0
-
-    lax.fori_loop(0, blocks, to_rows, 0, unroll=4)
-
-    def scatter(number, offset, count):
-        base = pl.multiple_of(number * count, count)
-        for k in range(0, count, batch):
-            rows = [sticks[pl.ds(base + k + j, 1), :] for j in range(batch)]
+    per_device = 2 * LANES
+    group = CHUNK // per_device
+    steps = blocks // group
+
+    def to_rows(step, slot):
+        for b in range(group):
+            i = lax.rem(step, steps) * group + b
+            block = jnp.concatenate([recv[i, k] for k in range(pieces)], axis=0)
+            block = jnp.concatenate([block, jnp.zeros((LANES - block.shape[0], LANES), jnp.float32)], axis=0)
+            turned = block.T
+            at = slot * CHUNK + b * per_device
+            sticks[at : at + LANES, :] = turned
+            sticks[at + LANES : at + per_device, :] = pltpu.roll(turned, LANES - values, 1)
+
+    to_rows(0, 0)
+
+    def scatter(step, slot):
+        to_rows(step + 1, 1 - slot)
+        for k in range(slot * CHUNK, (slot + 1) * CHUNK, batch):
+            rows = [sticks[k + j : k + j + 1, :] for j in range(batch)]
             for j in range(batch):
-                grid_rows[pl.ds(index[offset + k + j], 1), :] = rows[j]
-
-    walk(columns, index, index_sem, scatter)
+                grid_rows[pl.ds(index[k + j], 1), :] = rows[j]
+
+    walk(index_hbm, index, index_sem, scatter)
 
     def to_planes(u, _):
         turned = grid_rows[pl.ds(u * freqs, freqs), :].T
@@ -218,32 +227,44 @@
         return 0
 
     lax.fori_loop(0, freqs, to_planes, 0, unroll=8)
-
-
-def place_call(recv, columns, freqs):
-    chunk = 1024
+    position = lax.axis_index("fft")
+    mine = columns[pl.ds(position * 2, 2), :]
+    mine = jnp.concatenate([mine[0:1], mine[1:2]], axis=1)
+    centre = freqs // 2
+    along_u = jnp.floor((mine.astype(jnp.float32) + 0.5) * (1.0 / freqs)).astype(jnp.int32)
+    along_v = mine - along_u * freqs - centre
+    along_u = along_u - centre
+    along_w = lax.broadcasted_iota(jnp.int32, (freqs, mine.shape[1]), 0) - centre
+    squared = along_w * along_w + (along_u * along_u + along_v * along_v)
+    kinetic[...] = squared.astype(jnp.float32) * (0.5 / float(centre * centre))
+
+
+def place_call(recv, index, columns, freqs):
     tiles = -(-freqs // LANES)
     vmem = pl.BlockSpec(memory_space=pltpu.VMEM)
     anywhere = pl.BlockSpec(memory_space=pl.ANY)
     return pl.pallas_call(
         place_kernel,
-        out_shape=jax.ShapeDtypeStruct((tiles, freqs * ROWS, LANES), jnp.float32),
-        in_specs=[anywhere, vmem],
-        out_specs=vmem,
+        out_shape=(
+            jax.ShapeDtypeStruct((tiles, freqs * ROWS, LANES), jnp.float32),
+            jax.ShapeDtypeStruct((freqs, 2 * LANES), jnp.float32),
+        ),
+        in_specs=[anywhere, vmem, vmem],
+        out_specs=(vmem, vmem),
         scratch_shapes=[
-            pltpu.VMEM((columns.shape[0], LANES), jnp.float32),
+            pltpu.VMEM((2 * CHUNK, LANES), jnp.float32),
             pltpu.VMEM((freqs * freqs, LANES), jnp.float32),
-            pltpu.SMEM((2 * chunk,), jnp.int32),
+            pltpu.SMEM((2 * CHUNK,), jnp.int32),
             pltpu.SemaphoreType.DMA((2,)),
         ],
         compiler_params=pltpu.CompilerParams(vmem_limit_bytes=60 * 1024 * 1024),
         name="place",
-    )(columns, recv)
-
-
-def greet(position, count, own=None, bands=1):
+    )(index, columns.reshape(-1, LANES), recv)
+
+
+def greet(position, count, own=None, bands=1, hops=()):
     barrier = pltpu.get_barrier_semaphore()
-    for k in range(1, bands):
+    for k in hops:
         pl.semaphore_signal(barrier, inc=1, device_id={"band": lax.rem(own + k, bands)}, device_id_type=MESH)
 
     def signal(k, _):
@@ -340,7 +361,7 @@
     scale,
     weight,
     index_hbm,
-    columns,
+    within,
     psi_hbm,
     flat_hbm,
     potential_hbm,
@@ -350,7 +371,8 @@
     x_out_hbm,
     x_back_hbm,
     y_back_hbm,
-    hpsi,
+    kinetic_hbm,
+    local,
     margin,
     psi,
     flat,
@@ -361,7 +383,9 @@
     x_out,
     x_back,
     y_back,
+    kinetic,
     others,
+    far,
     planes,
     grid_rows,
     sticks,
@@ -374,16 +398,19 @@
     load_sem,
     band_send_sem,
     band_recv_sem,
+    far_send_sem,
+    far_recv_sem,
     send_sem,
     recv_sem,
     sum_send_sem,
     sum_recv_sem,
 ):
-    bands = others.shape[0] + 1
+    bands = others.shape[0] + 2
+    hops = (1, bands - 1)
     count, pieces, depth, _ = got.shape
     values = pieces * depth // 2
-    freqs = hpsi.shape[2]
-    per_device = hpsi.shape[3]
+    freqs = local.shape[2]
+    per_device = local.shape[3]
     batch = 64
     position = lax.axis_index("fft")
     own = lax.axis_index("band")
@@ -398,52 +425,77 @@
             (psi_hbm, psi),
             (high_hbm, table_high),
             (low_hbm, table_low),
+            (kinetic_hbm, kinetic),
         ),
         load_sem,
     )
-    barrier = greet(position, count, own, bands)
-    pl.semaphore_wait(barrier, count + bands - 2)
+    barrier = greet(position, count, own, bands, hops)
+    pl.semaphore_wait(barrier, count - 1 + len(hops))
     band_copies = [
         pltpu.make_async_remote_copy(
             src_ref=psi_hbm,
-            dst_ref=others.at[k - 1],
-            send_sem=band_send_sem.at[k - 1],
-            recv_sem=band_recv_sem.at[k - 1],
+            dst_ref=others.at[at],
+            send_sem=band_send_sem.at[at],
+            recv_sem=band_recv_sem.at[at],
             device_id={"band": lax.rem(own + bands - k, bands)},
             device_id_type=MESH,
         )
-        for k in range(1, bands)
+        for at, k in enumerate(hops)
     ]
     for copy in band_copies:
         copy.start()
     for load in loads:
         load.wait()
     through_planes(flat, planes, potential, y_out, x_out, x_back, y_back)
-
-    def from_planes(u, _):
+    for copy in band_copies:
+        copy.wait()
+    far_copies = [
+        pltpu.make_async_remote_copy(
+            src_ref=others.at[at, pl.ds(at * freqs, freqs)],
+            dst_ref=far.at[pl.ds(at * freqs, freqs)],
+            send_sem=far_send_sem.at[at],
+            recv_sem=far_recv_sem.at[at],
+            device_id={"band": lax.rem(own + bands - k, bands)},
+            device_id_type=MESH,
+        )
+        for at, k in enumerate(hops)
+    ]
+    for copy in far_copies:
+        copy.start()
+
+    def from_planes(i, _):
         for k in range(planes.shape[0]):
             upper = min(freqs - k * LANES, LANES)
-            turned = planes[k, pl.ds(u, ROWS, stride=freqs), :].T
-            grid_rows[pl.ds(u * freqs + k * LANES, upper), 0:ROWS] = turned[:upper]
-        return 0
-
-    lax.fori_loop(0, freqs, from_planes, 0, unroll=8)
-
-    def gather(number, offset, length):
-        for k in range(0, length, batch):
-            rows = [grid_rows[pl.ds(index[offset + k + j], 1), :] for j in range(batch)]
-            for j in range(batch):
-                sticks[pl.ds(offset + k + j, 1), :] = rows[j]
-        group = length // per_device
+            rows = [planes[k, pl.ds(i * PACK + j, ROWS, stride=freqs), :] for j in range(PACK)]
+            rows = jnp.concatenate(rows, axis=0).T
+            grid_rows[pl.ds(i * freqs + k * LANES, upper), 0 : PACK * ROWS] = rows[:upper]
+        return 0
+
+    lax.fori_loop(0, freqs // PACK, from_planes, 0, unroll=4)
+    group = CHUNK // per_device
+    steps = count // group
+    first = lax.div(position, group) + 1
+    sticks[CHUNK : 2 * CHUNK, :] = jnp.zeros((CHUNK, LANES), jnp.float32)
+
+    def turned(at, line):
+        rows = sticks[at : at + LANES, :].T
+        place = within[pl.ds(line, 1), :]
+        total = jnp.zeros((ROWS, LANES), jnp.float32)
+        for k in range(PACK):
+            total = jnp.where(place == k, rows[k * ROWS : (k + 1) * ROWS], total)
+        return total[:values]
+
+    def turn(step, slot):
         for k in range(group):
-            at = offset + k * per_device
-            first = sticks[pl.ds(at, LANES), :].T[:values]
-            second = sticks[pl.ds(at + LANES, LANES), :].T[:values]
-            block = jnp.concatenate([first, second], axis=0)
+            peer = lax.rem(first + step, steps) * group + k
+            at = slot * CHUNK + k * per_device
+            block = jnp.concatenate([turned(at, peer * 2), turned(at + LANES, peer * 2 + 1)], axis=0)
             for piece in range(pieces):
-                send[number * group + k, piece] = block[piece * depth : (piece + 1) * depth]
+                send[peer, piece] = block[piece * depth : (piece + 1) * depth]
+
+    def post(step):
         for k in range(group):
-            peer = number * group + k
+            peer = lax.rem(first + step, steps) * group + k
 
             @pl.when(peer != position)
             def _(peer=peer):
@@ -456,18 +508,21 @@
                     device_id_type=MESH,
                 ).start()
 
-    chunk = index.shape[0] // 2
-    walk(index_hbm, index, index_sem, gather, lax.div(position * per_device, chunk) + 1)
+    def gather(step, slot):
+        for k in range(slot * CHUNK, (slot + 1) * CHUNK, batch):
+            rows = [grid_rows[pl.ds(index[k + j], 1), :] for j in range(batch)]
+            for j in range(batch):
+                sticks[k + j : k + j + 1, :] = rows[j]
+        turn(step + steps - 1, 1 - slot)
+
+        @pl.when(step > 0)
+        def _():
+            post(step + steps - 1)
+
+    walk(index_hbm, index, index_sem, gather, first)
+    turn(steps - 1, 1)
+    post(steps - 1)
     got[position] = send[position]
-    mine = columns[pl.ds(position * 2, 2), :]
-    mine = jnp.concatenate([mine[0:1], mine[1:2]], axis=1)
-    centre = freqs // 2
-    along_u = jnp.floor((mine.astype(jnp.float32) + 0.5) * (1.0 / freqs)).astype(jnp.int32)
-    along_v = mine - along_u * freqs - centre
-    along_u = along_u - centre
-    along_w = lax.broadcasted_iota(jnp.int32, (freqs, mine.shape[1]), 0) - centre
-    squared = along_w * along_w + (along_u * along_u + along_v * along_v)
-    kinetic = squared.astype(jnp.float32) * (0.5 / float(centre * centre))
     await_others(got, recv_sem)
 
     def to_right(i, _):
@@ -481,21 +536,22 @@
     lax.fori_loop(0, count, to_right, 0, unroll=4)
     high, low = split(right[...])
     applied = dot(table_high[...], high) + dot(table_low[...], high) + dot(table_high[...], low)
-    right_re = kinetic * psi[0:freqs, :] + applied[:freqs] * scale
-    right_im = kinetic * psi[freqs : 2 * freqs, :] + applied[freqs:] * scale
-    hpsi[0, 0] = right_re
-    hpsi[1, 0] = right_im
+    applied = applied * scale
+    local[0, 0] = applied[:freqs]
+    local[1, 0] = applied[freqs:]
+    right_re = kinetic[...] * psi[0:freqs, :] + applied[:freqs]
+    right_im = kinetic[...] * psi[freqs : 2 * freqs, :] + applied[freqs:]
 
     def folded(product):
         narrow = product[:, :LANES] + product[:, LANES:]
         return jnp.sum(narrow, axis=0, keepdims=True)
 
-    for copy in band_copies:
+    for copy in far_copies:
         copy.wait()
     line = lax.broadcasted_iota(jnp.int32, (2 * bands, LANES), 0)
     tile = jnp.zeros((2 * bands, LANES), jnp.float32)
     for k in range(bands):
-        left = psi if k == 0 else others.at[k - 1]
+        left = psi if k == 0 else others.at[hops.index(k)] if k in hops else far
         left_re, left_im = left[0:freqs, :], left[freqs : 2 * freqs, :]
         row = lax.rem(own + k, bands)
         tile = jnp.where(line == row, folded(left_re * right_re + left_im * right_im), tile)
@@ -515,41 +571,45 @@
 
     lax.fori_loop(1, count, post_sums, 0)
     await_others(sums, sum_recv_sem)
-    margin[...] = jnp.sum(jnp.sum(sums[...], axis=0), axis=1, keepdims=True)
+    result = jnp.sum(jnp.sum(sums[...], axis=0).T, axis=0, keepdims=True)
+    margin[0] = result[:, :bands]
+    margin[1] = result[:, bands:]
     await_others(got, send_sem)
     await_others(sums, sum_send_sem)
 
 
-def collect_call(flat, potential, renumbered, columns, psi, table, cosine, sine, scale, weight, shape, count, bands):
+def collect_call(flat, kinetic, potential, index, within, psi, table, cosine, sine, scale, weight, shape, count, bands):
     freqs = cosine.shape[1]
     planes_held = potential.shape[0]
     vmem = pl.BlockSpec(memory_space=pltpu.VMEM)
     anywhere = pl.BlockSpec(memory_space=pl.ANY)
-    chunk = 1024
     table = table.T
     tables = plane_tables(cosine, sine)
     blocks = (count, planes_held, 2 * psi.shape[1] // LANES, LANES)
-    operands = (psi, flat, potential, *halves(table), *tables)
+    operands = (psi, flat, potential, *halves(table), *tables, kinetic)
     return pl.pallas_call(
         functools.partial(collect_kernel, scale, weight),
-        out_shape=(jax.ShapeDtypeStruct(shape, jnp.float32), jax.ShapeDtypeStruct((2 * bands, 1), jnp.float32)),
+        out_shape=(jax.ShapeDtypeStruct(shape, jnp.float32), jax.ShapeDtypeStruct((2, 1, bands), jnp.float32)),
         in_specs=[anywhere, vmem] + [anywhere] * len(operands),
         out_specs=(vmem, vmem),
         scratch_shapes=[
             *[pltpu.VMEM(operand.shape, operand.dtype) for operand in operands],
-            pltpu.VMEM((bands - 1, *psi.shape), jnp.float32),
+            pltpu.VMEM((2, *psi.shape), jnp.float32),
+            pltpu.VMEM(psi.shape, jnp.float32),
             pltpu.VMEM((flat.shape[0], ROWS * freqs, LANES), jnp.float32),
-            pltpu.VMEM((freqs * freqs, LANES), jnp.float32),
-            pltpu.VMEM((2 * chunk, LANES), jnp.float32),
+            pltpu.VMEM((freqs // PACK * freqs, LANES), jnp.float32),
+            pltpu.VMEM((2 * CHUNK, LANES), jnp.float32),
             pltpu.VMEM(blocks, jnp.float32),
             pltpu.VMEM(blocks, jnp.float32),
             pltpu.VMEM((count * ROWS, psi.shape[1]), jnp.float32),
             pltpu.VMEM((count, 2 * bands, LANES), jnp.float32),
-            pltpu.SMEM((2 * chunk,), jnp.int32),
+            pltpu.SMEM((2 * CHUNK,), jnp.int32),
             pltpu.SemaphoreType.DMA((2,)),
             pltpu.SemaphoreType.DMA((len(operands),)),
-            pltpu.SemaphoreType.DMA((bands - 1,)),
-            pltpu.SemaphoreType.DMA((bands - 1,)),
+            pltpu.SemaphoreType.DMA((2,)),
+            pltpu.SemaphoreType.DMA((2,)),
+            pltpu.SemaphoreType.DMA((2,)),
+            pltpu.SemaphoreType.DMA((2,)),
             pltpu.SemaphoreType.DMA,
             pltpu.SemaphoreType.DMA,
             pltpu.SemaphoreType.DMA,
@@ -559,7 +619,7 @@
             collective_id=1, has_side_effects=True, vmem_limit_bytes=60 * 1024 * 1024
         ),
         name="collect",
-    )(renumbered, columns.reshape(-1, LANES), *operands)
+    )(index, within.reshape(-1, LANES), *operands)
 
 
 def on_device(psi, potential, stick_columns):
@@ -576,18 +636,24 @@
     flat_psi = psi.reshape(2 * freq_count, per_device)
     moved = spread_call(flat_psi, table, fft_count, plane_count)
     bands = lax.axis_size("band")
-    along_v = stick_columns % freq_count
-    along_u = stick_columns // freq_count
-    along_u = along_u % 2 * (freq_count // 2) + along_u // 2
-    renumbered = along_u * freq_count + along_v
-    flat = place_call(moved, renumbered, freq_count)
+    if freq_count == 160:
+        fives = lax.shift_right_logical(stick_columns, 5)
+        along_u = lax.shift_right_logical(fives * 52429, 18)
+    else:
+        along_u = stick_columns // freq_count
+    along_v = stick_columns - along_u * freq_count
+    along_u = (along_u & 1) * (freq_count // 2) + lax.shift_right_logical(along_u, 1)
+    out_index = along_u * freq_count + along_v
+    back_index = lax.shift_right_logical(along_u, PACK.bit_length() - 1) * freq_count + along_v
+    flat, kinetic = place_call(moved, out_index, stick_columns, freq_count)
     scale = 1.0 / float(grid_size * grid_size * grid_size)
     weight = 1.0 / float(freq_count * per_device * fft_count)
-    hpsi, margin = collect_call(
+    applied, margin = collect_call(
         flat,
+        kinetic,
         potential,
-        renumbered,
-        stick_columns,
+        back_index,
+        along_u & (PACK - 1),
         flat_psi,
         table,
         cosine,
@@ -598,7 +664,7 @@
         fft_count,
         bands,
     )
-    return (hpsi, margin.reshape(2, bands, 1))
+    return (kinetic * psi + applied, margin.swapaxes(1, 2))
 
 
 def solution(mesh):

time: 103 us -> 98.8 us (0.959)
  Pallas kernels: 96.8 us -> 92.4 us
  local copies, waits for them, and re-layouts: 2.36 us -> 1.21 us
    pallas_call x1, Pallas kernels: 22.6 us -> 19.2 us  [place_call(): pl.pallas_call(place_kernel, out_shape=(jax.ShapeDtypeStruct((tiles, freq...]
    add x1 -> x2, other arithmetic: 1.6 us -> 3.31 us  [the longest x1 1.75 us: on_device(): return (kinetic * psi + applied, margin.swapaxes(1, 2))]
    pallas_call x1, Pallas kernels: 55.2 us -> 54.1 us  [collect_call(): pl.pallas_call(functools.partial(collect_kernel, scale, weight), out_shap...]
where the time goes in v4:
time: 98.8 us; the launch traced here: 97.6 us
  Pallas kernels  92.4 us (94%)
  other arithmetic  3.31 us (3%)
  local copies, waits for them, and re-layouts  1.21 us (1%)
    pallas_call x1, Pallas kernels, collect_call(): pl.pallas_call(functools.partial(collect_kernel, scale, weight), out_shap...  54.1 us
    pallas_call x1, Pallas kernels, place_call(): pl.pallas_call(place_kernel, out_shape=(jax.ShapeDtypeStruct((tiles, freq...  19.2 us
    pallas_call x1, Pallas kernels, spread_call(): pl.pallas_call(spread_kernel, out_shape=jax.ShapeDtypeStruct(shape, jnp.f...  19.1 us

profile of v4, /device:TPU:1, one launch (start us, length us, event | category | flops | bytes accessed | tf_op | source)
XLA Modules:
  0.0 97.6 jit_solution(9740334827605656357)
XLA Ops:
  0.6 1.6 %multiply_add_fusion.2 = (s32[16384]{0:T(1024)}, s32[16384]{0:T(1024)}, s32[128,128]{1,0:T(8,128)}) fusion(s32[16384]{0:T(1024)} %param.13), kind=kLoop, calls=%fused_computation.4 | loop fusion | flops 245760 | bytes 262144 | tf_op jit(solution)/shard_map/add | solution.py:646
  2.2 19.1 %spread.1.recv = f32[64,5,4,128]{3,2,1,0:T(4,128)} custom-call(f32[320,256]{1,0:T(8,128)} %bitcast.7, bf16[1024,320]{1,0:T(8,128)(2,1)} %constant.32.clone.high_hbm, bf16[1024,320]{1,0:T(8,128)(2,1)} %constant.33.clone.low_hbm), custom_call_target="tpu_custom_call" | custom-call | tf_op jit(solution)/shard_map/spread/pallas_call | solution.py:338
  21.3 19.2 %place.1 = (f32[2,2560,128]{2,1,0:T(8,128)}, f32[160,256]{1,0:T(8,128)}) custom-call(s32[16384]{0:T(1024)} %get-tuple-element.12.index_hbm, s32[128,128]{1,0:T(8,128)} %bitcast.9, f32[64,5,4,128]{3,2,1,0:T(4,128)} %spread.1.recv), custom_call_target="tpu_custom_call" | custom-call | tf_op jit(solution)/shard_map/place/pallas_call | solution.py:246
  40.6 0.0 copy-start
  40.6 0.0 copy-start.1
  40.6 54.1 %collect.1 = (f32[2,1,160,256]{3,2,1,0:T(8,128)}, f32[2,1,4]{2,1,0:T(1,128)}) custom-call(s32[16384]{0:T(1024)} %get-tuple-element.13.index_hbm, s32[128,128]{1,0:T(8,128)} %get-tuple-element.14.within, f32[320,256]{1,0:T(8,128)} %bitcast.8, f32[2,2560,128]{2,1,0:T(8,128)} %get-tuple-element.7.flat_hbm, f32[5,320,320]{2,1,0:T(8,128)} %potential_hbm.1, ...), custom_call_target="tpu_custom_call" | custom-call | tf_op jit(solution)/shard_map/collect/pallas_call | solution.py:590
  94.7 0.0 copy-done
  94.7 0.0 copy-done.1
  94.7 1.7 %multiply_add_fusion = f32[2,1,160,256]{3,2,1,0:T(8,128)} fusion(f32[2,1,160,256]{3,2,1,0:T(8,128)} %get-tuple-element.8, f32[2,1,160,256]{3,2,1,0:T(8,128)S(1)} %copy-done, f32[160,256]{1,0:T(8,128)S(1)} %copy-done.1), kind=kLoop, calls=%fused_computation | loop fusion | flops 163840 | bytes 1146880 | tf_op jit(solution)/shard_map/add | solution.py:667
  96.4 1.2 %copy.15 = f32[2,4,1]{1,2,0:T(1,128)} copy(f32[2,4,1]{1,2,0:T(1,128)} %bitcast.10) | data formatting | bytes 64
Async XLA Ops:
  40.6 54.1 %copy-start = (f32[2,1,160,256]{3,2,1,0:T(8,128)S(1)}, f32[2,1,160,256]{3,2,1,0:T(8,128)}, u32[]{:S(2)}) copy-start(f32[2,1,160,256]{3,2,1,0:T(8,128)} %param.11) | copy-start | bytes 983044
  40.6 54.1 %copy-start.1 = (f32[160,256]{1,0:T(8,128)S(1)}, f32[160,256]{1,0:T(8,128)}, u32[]{:S(2)}) copy-start(f32[160,256]{1,0:T(8,128)} %get-tuple-element.6.kinetic_hbm) | copy-start | bytes 491524

commit v5 on v4

--- a/solution.py
+++ b/solution.py
@@ -447,6 +447,66 @@
     for load in loads:
         load.wait()
     through_planes(flat, planes, potential, y_out, x_out, x_back, y_back)
+
+    def from_planes(i, _):
+        for k in range(planes.shape[0]):
+            upper = min(freqs - k * LANES, LANES)
+            rows = [planes[k, pl.ds(i * PACK + j, ROWS, stride=freqs), :] for j in range(PACK)]
+            rows = jnp.concatenate(rows, axis=0).T
+            grid_rows[pl.ds(i * freqs + k * LANES, upper), 0 : PACK * ROWS] = rows[:upper]
+        return 0
+
+    lax.fori_loop(0, freqs // PACK, from_planes, 0, unroll=4)
+    group = CHUNK // per_device
+    steps = count // group
+    first = lax.div(position, group) + 1
+    sticks[CHUNK : 2 * CHUNK, :] = jnp.zeros((CHUNK, LANES), jnp.float32)
+
+    def turned(at, line):
+        rows = sticks[at : at + LANES, :].T
+        place = within[pl.ds(line, 1), :]
+        total = jnp.zeros((ROWS, LANES), jnp.float32)
+        for k in range(PACK):
+            total = jnp.where(place == k, rows[k * ROWS : (k + 1) * ROWS], total)
+        return total[:values]
+
+    def turn(step, slot):
+        for k in range(group):
+            peer = lax.rem(first + step, steps) * group + k
+            at = slot * CHUNK + k * per_device
+            block = jnp.concatenate([turned(at, peer * 2), turned(at + LANES, peer * 2 + 1)], axis=0)
+            for piece in range(pieces):
+                send[peer, piece] = block[piece * depth : (piece + 1) * depth]
+
+    def post(step):
+        for k in range(group):
+            peer = lax.rem(first + step, steps) * group + k
+
+            @pl.when(peer != position)
+            def _(peer=peer):
+                pltpu.make_async_remote_copy(
+                    src_ref=send.at[peer],
+                    dst_ref=got.at[position],
+                    send_sem=send_sem,
+                    recv_sem=recv_sem,
+                    device_id={"fft": peer},
+                    device_id_type=MESH,
+                ).start()
+
+    def gather(step, slot):
+        for k in range(slot * CHUNK, (slot + 1) * CHUNK, batch):
+            rows = [grid_rows[pl.ds(index[k + j], 1), :] for j in range(batch)]
+            for j in range(batch):
+                sticks[k + j : k + j + 1, :] = rows[j]
+        turn(step + steps - 1, 1 - slot)
+
+        @pl.when(step > 0)
+        def _():
+            post(step + steps - 1)
+
+    walk(index_hbm, index, index_sem, gather, first)
+    turn(steps - 1, 1)
+    post(steps - 1)
     for copy in band_copies:
         copy.wait()
     far_copies = [
@@ -462,66 +522,6 @@
     ]
     for copy in far_copies:
         copy.start()
-
-    def from_planes(i, _):
-        for k in range(planes.shape[0]):
-            upper = min(freqs - k * LANES, LANES)
-            rows = [planes[k, pl.ds(i * PACK + j, ROWS, stride=freqs), :] for j in range(PACK)]
-            rows = jnp.concatenate(rows, axis=0).T
-            grid_rows[pl.ds(i * freqs + k * LANES, upper), 0 : PACK * ROWS] = rows[:upper]
-        return 0
-
-    lax.fori_loop(0, freqs // PACK, from_planes, 0, unroll=4)
-    group = CHUNK // per_device
-    steps = count // group
-    first = lax.div(position, group) + 1
-    sticks[CHUNK : 2 * CHUNK, :] = jnp.zeros((CHUNK, LANES), jnp.float32)
-
-    def turned(at, line):
-        rows = sticks[at : at + LANES, :].T
-        place = within[pl.ds(line, 1), :]
-        total = jnp.zeros((ROWS, LANES), jnp.float32)
-        for k in range(PACK):
-            total = jnp.where(place == k, rows[k * ROWS : (k + 1) * ROWS], total)
-        return total[:values]
-
-    def turn(step, slot):
-        for k in range(group):
-            peer = lax.rem(first + step, steps) * group + k
-            at = slot * CHUNK + k * per_device
-            block = jnp.concatenate([turned(at, peer * 2), turned(at + LANES, peer * 2 + 1)], axis=0)
-            for piece in range(pieces):
-                send[peer, piece] = block[piece * depth : (piece + 1) * depth]
-
-    def post(step):
-        for k in range(group):
-            peer = lax.rem(first + step, steps) * group + k
-
-            @pl.when(peer != position)
-            def _(peer=peer):
-                pltpu.make_async_remote_copy(
-                    src_ref=send.at[peer],
-                    dst_ref=got.at[position],
-                    send_sem=send_sem,
-                    recv_sem=recv_sem,
-                    device_id={"fft": peer},
-                    device_id_type=MESH,
-                ).start()
-
-    def gather(step, slot):
-        for k in range(slot * CHUNK, (slot + 1) * CHUNK, batch):
-            rows = [grid_rows[pl.ds(index[k + j], 1), :] for j in range(batch)]
-            for j in range(batch):
-                sticks[k + j : k + j + 1, :] = rows[j]
-        turn(step + steps - 1, 1 - slot)
-
-        @pl.when(step > 0)
-        def _():
-            post(step + steps - 1)
-
-    walk(index_hbm, index, index_sem, gather, first)
-    turn(steps - 1, 1)
-    post(steps - 1)
     got[position] = send[position]
     await_others(got, recv_sem)
 

time: 98.8 us -> 97.3 us (0.985)
  Pallas kernels: 92.4 us -> 91 us
    pallas_call x1, Pallas kernels: 54.1 us -> 52.6 us  [collect_call(): pl.pallas_call(functools.partial(collect_kernel, scale, weight), out_shap...]
where the time goes in v5:
time: 97.3 us; the launch traced here: 96.2 us
  Pallas kernels  91 us (94%)
  other arithmetic  3.31 us (3%)
  local copies, waits for them, and re-layouts  1.21 us (1%)
    pallas_call x1, Pallas kernels, collect_call(): pl.pallas_call(functools.partial(collect_kernel, scale, weight), out_shap...  52.6 us
    pallas_call x1, Pallas kernels, place_call(): pl.pallas_call(place_kernel, out_shape=(jax.ShapeDtypeStruct((tiles, freq...  19.2 us
    pallas_call x1, Pallas kernels, spread_call(): pl.pallas_call(spread_kernel, out_shape=jax.ShapeDtypeStruct(shape, jnp.f...  19.1 us

profile of v5, /device:TPU:1, one launch (start us, length us, event | category | flops | bytes accessed | tf_op | source)
XLA Modules:
  0.0 96.2 jit_solution(6589920845361865729)
XLA Ops:
  0.6 1.6 %multiply_add_fusion.2 = (s32[16384]{0:T(1024)}, s32[16384]{0:T(1024)}, s32[128,128]{1,0:T(8,128)}) fusion(s32[16384]{0:T(1024)} %param.13), kind=kLoop, calls=%fused_computation.4 | loop fusion | flops 245760 | bytes 262144 | tf_op jit(solution)/shard_map/add | solution.py:646
  2.2 19.1 %spread.1.recv = f32[64,5,4,128]{3,2,1,0:T(4,128)} custom-call(f32[320,256]{1,0:T(8,128)} %bitcast.7, bf16[1024,320]{1,0:T(8,128)(2,1)} %constant.32.clone.high_hbm, bf16[1024,320]{1,0:T(8,128)(2,1)} %constant.33.clone.low_hbm), custom_call_target="tpu_custom_call" | custom-call | tf_op jit(solution)/shard_map/spread/pallas_call | solution.py:338
  21.3 19.2 %place.1 = (f32[2,2560,128]{2,1,0:T(8,128)}, f32[160,256]{1,0:T(8,128)}) custom-call(s32[16384]{0:T(1024)} %get-tuple-element.12.index_hbm, s32[128,128]{1,0:T(8,128)} %bitcast.9, f32[64,5,4,128]{3,2,1,0:T(4,128)} %spread.1.recv), custom_call_target="tpu_custom_call" | custom-call | tf_op jit(solution)/shard_map/place/pallas_call | solution.py:246
  40.6 0.0 copy-start
  40.6 0.0 copy-start.1
  40.6 52.6 %collect.1 = (f32[2,1,160,256]{3,2,1,0:T(8,128)}, f32[2,1,4]{2,1,0:T(1,128)}) custom-call(s32[16384]{0:T(1024)} %get-tuple-element.13.index_hbm, s32[128,128]{1,0:T(8,128)} %get-tuple-element.14.within, f32[320,256]{1,0:T(8,128)} %bitcast.8, f32[2,2560,128]{2,1,0:T(8,128)} %get-tuple-element.7.flat_hbm, f32[5,320,320]{2,1,0:T(8,128)} %potential_hbm.1, ...), custom_call_target="tpu_custom_call" | custom-call | tf_op jit(solution)/shard_map/collect/pallas_call | solution.py:590
  93.2 0.0 copy-done
  93.2 0.0 copy-done.1
  93.2 1.7 %multiply_add_fusion = f32[2,1,160,256]{3,2,1,0:T(8,128)} fusion(f32[2,1,160,256]{3,2,1,0:T(8,128)} %get-tuple-element.8, f32[2,1,160,256]{3,2,1,0:T(8,128)S(1)} %copy-done, f32[160,256]{1,0:T(8,128)S(1)} %copy-done.1), kind=kLoop, calls=%fused_computation | loop fusion | flops 163840 | bytes 1146880 | tf_op jit(solution)/shard_map/add | solution.py:667
  95.0 1.2 %copy.15 = f32[2,4,1]{1,2,0:T(1,128)} copy(f32[2,4,1]{1,2,0:T(1,128)} %bitcast.10) | data formatting | bytes 64
Async XLA Ops:
  40.6 52.6 %copy-start = (f32[2,1,160,256]{3,2,1,0:T(8,128)S(1)}, f32[2,1,160,256]{3,2,1,0:T(8,128)}, u32[]{:S(2)}) copy-start(f32[2,1,160,256]{3,2,1,0:T(8,128)} %param.11) | copy-start | bytes 983044
  40.6 52.6 %copy-start.1 = (f32[160,256]{1,0:T(8,128)S(1)}, f32[160,256]{1,0:T(8,128)}, u32[]{:S(2)}) copy-start(f32[160,256]{1,0:T(8,128)} %get-tuple-element.6.kinetic_hbm) | copy-start | bytes 491524
